TPU v7x, 256 devices: a whole 4x4x8 slice. The times are simulated.
256 devices in a mesh: dp: 128 (over z, y, x_lo, core), mp: 2 (over x_hi).
Axes of the slice: x: 4 (x_hi: 2, x_lo: 2; x = x_hi * 2 + x_lo), y: 4, z: 8, core: 2. Of those that a mesh axis runs over, the one named last changes fastest.
Arguments:
- head_hidden: bfloat16 [16384, 2048], P('dp'), may hold values from -30 to 30
- proj_weight: bfloat16 [2048, 512], P(None, 'mp'), may hold values from -0.125 to 0.125
- pair_perm: int32 [8192], replicated, may hold values from 0 to 8191, as said below
Outputs:
- mean_contrast_cost: float32 [], replicated
- grad_emb: float32 [16384, 512], P('dp', 'mp')
- grad_proj: float32 [2048, 512], P(None, 'mp')
Inputs may be any that keep to these rules, and one draw needn't show every extreme that they name: `pair_perm`: every number of 0 to 8191 appears once.
All inputs are finite; a program needn't handle non-finite values.
Results may differ from a plain program's by a relative error of at most 0.0079.
Values may be sent and summed in bfloat16 or wider, within the bound.
A program may use at most 64 MiB of HBM per device.

v0:
```python
import jax
import jax.numpy as jnp
from jax import lax
from jax.sharding import PartitionSpec as P

inverse_sharpness_factor = 10.0


def column_rows(col_count, share_rows, own_rows, offset):
    positions = jnp.arange(col_count, dtype=jnp.int32)
    return positions // share_rows * own_rows + offset + positions % share_rows


def scores(unitlength_vectors, block):
    return lax.dot_general(
        unitlength_vectors, block, (((1,), (1,)), ((), ())), preferred_element_type=jnp.float32
    )


def per_device(head_hidden, proj_weight, pair_perm):
    own_rows = head_hidden.shape[0]
    groups = lax.axis_size("mp")
    share_rows = own_rows // groups
    dp_index = lax.axis_index("dp")
    mp_index = lax.axis_index("mp")
    embed_part = jnp.dot(head_hidden, proj_weight, preferred_element_type=jnp.float32).astype(
        jnp.bfloat16
    )
    embed_full = lax.all_gather(embed_part, "mp", axis=1, tiled=True)
    embed_float = embed_full.astype(jnp.float32)
    inverse_norm = lax.rsqrt(jnp.sum(embed_float * embed_float, axis=1) + 1e-06)
    unitlength_vectors = (embed_float * inverse_norm[:, None]).astype(jnp.bfloat16)
    source_positions = dp_index * own_rows + jnp.arange(own_rows, dtype=jnp.int32)
    half_rows = pair_perm.shape[0]
    first_start = jnp.minimum(dp_index * own_rows, half_rows - own_rows)
    forward_pair = half_rows + lax.dynamic_slice_in_dim(pair_perm, first_start, own_rows)
    matches = pair_perm[None, :] == (source_positions - half_rows)[:, None]
    backward_pair = jnp.sum(
        jnp.where(matches, jnp.arange(half_rows, dtype=jnp.int32)[None, :], 0), axis=1
    )
    partner = jnp.where(source_positions < half_rows, forward_pair, backward_pair)
    offset = mp_index * share_rows
    own_half = lax.dynamic_slice_in_dim(unitlength_vectors, offset, share_rows, 0)
    block = lax.all_gather(own_half, "dp", axis=0, tiled=True)
    target_positions = column_rows(block.shape[0], share_rows, own_rows, offset)
    angle_agreement = scores(unitlength_vectors, block)
    exponentiated_terms = jnp.where(
        target_positions[None, :] == source_positions[:, None],
        0.0,
        jnp.exp(inverse_sharpness_factor * (angle_agreement - 1.0)),
    )
    positive_hit = jnp.where(target_positions[None, :] == partner[:, None], angle_agreement, 0.0)
    totals = jnp.sum(exponentiated_terms, axis=1)
    matched_pair_logit = jnp.sum(positive_hit, axis=1)
    totals, matched_pair_logit = lax.psum((totals, matched_pair_logit), "mp")
    log_partition_entries = jnp.log(totals)
    sample_cost_vector = log_partition_entries - inverse_sharpness_factor * (
        matched_pair_logit - 1.0
    )
    log_half = lax.dynamic_slice_in_dim(log_partition_entries, offset, share_rows, 0)
    far_logs_all = lax.all_gather(log_half, "dp", axis=0, tiled=True)
    block = lax.all_gather(own_half, "dp", axis=0, tiled=True)
    col_count = block.shape[0]
    target_positions = column_rows(col_count, share_rows, own_rows, offset)
    angle_agreement = scores(unitlength_vectors, block)
    stabilized_logits = inverse_sharpness_factor * (angle_agreement - 1.0)
    projection_matrix_piece = jnp.exp(stabilized_logits - log_partition_entries[:, None]) + jnp.exp(
        stabilized_logits - far_logs_all[None, :]
    )
    projection_matrix_piece = jnp.where(
        target_positions[None, :] == source_positions[:, None], 0.0, projection_matrix_piece
    )
    projection_matrix_piece = projection_matrix_piece - jnp.where(
        target_positions[None, :] == partner[:, None], 2.0, 0.0
    )
    incomplete_derivative = jnp.dot(
        projection_matrix_piece.astype(jnp.bfloat16), block, preferred_element_type=jnp.float32
    )
    col_width = embed_part.shape[1]
    unitvec_derivative = inverse_sharpness_factor * lax.psum(incomplete_derivative, "mp")
    inner_dots = jnp.sum(embed_float * unitvec_derivative, axis=1)
    full_grad = (
        inverse_norm[:, None] * unitvec_derivative
        - embed_float * (inverse_norm**3 * inner_dots)[:, None]
    )
    grad_emb = lax.dynamic_slice_in_dim(full_grad, mp_index * col_width, col_width, 1)
    weight_part = lax.dot_general(
        head_hidden,
        grad_emb.astype(jnp.bfloat16),
        (((0,), (0,)), ((), ())),
        preferred_element_type=jnp.float32,
    )
    grad_proj, loss_total = lax.psum((weight_part, jnp.sum(sample_cost_vector)), "dp")
    mean_contrast_cost = loss_total / (own_rows * lax.axis_size("dp"))
    return (mean_contrast_cost, grad_emb, grad_proj)


def solution(mesh):
    placed = (P("dp", None), P(None, "mp"), P())
    return jax.shard_map(
        per_device,
        mesh=mesh,
        in_specs=placed,
        out_specs=(P(), P("dp", "mp"), P(None, "mp")),
        check_vma=False,
    )
```

profile of v0, /device:TPU:1, one launch (start us, length us, event | category | flops | bytes accessed | tf_op | source)
XLA Modules:
  0.0 1948.8 jit_solution(6093067086970455723)
XLA Ops:
  7.2 1.2 copy-done
  8.4 1.3 convolution_convert_fusion
  9.7 5.9 all_gather.10
  15.6 0.1 multiply_reduce_fusion.1
  15.8 0.1 multiply_convert_fusion
  15.9 0.6 constant_dynamic-slice_fusion
  16.5 0.0 all-reduce.6.cloned.1.call-start
  16.6 1.3 dynamic-slice
  18.5 1.5 select_reduce_fusion
  20.0 0.8 compare_select_fusion.4
  20.8 220.0 %all-gather.2.cloned.1.call-done = bf16[8192,512]{1,0:T(8,128)(2,1)} async-done(((bf16[64,512]{1,0:T(8,128)(2,1)}), bf16[8192,512]{1,0:T(8,128)(2,1)}) %all-gather.2.cloned.1.call-update) | async-done | bytes 8388624 | tf_op jit(solution)/shard_map/all_gather | solution.py:44
  240.8 8.3 fusion
  249.1 5.3 all-reduce.2
  254.4 0.6 fusion.25
  255.0 0.2 dynamic-slice_dynamic-update-slice_fusion
  255.2 544.6 %all-reduce.1 = (f32[]{:T(128)}, f32[8192]{0:T(1024)S(1)}) all-reduce(f32[]{:T(128)} %get-tuple-element.18, f32[8192]{0:T(1024)S(1)} %dynamic-slice_dynamic-update-slice_fusion), channel_id=1, replica_groups=mesh['dp'=128,'mp'=2] {'dp'}, use_global_device_ids=true, to_apply=%region_7.8 | all-reduce | flops 8193 | bytes 65544 | tf_op jit(solution)/shard_map/psum | solution.py:93
  799.8 7.6 fusion.4
  807.4 0.0 all-reduce.8.cloned.1.call-start
  807.5 39.2 %all-reduce.6.cloned.1.call-done = f32[128,512]{1,0:T(8,128)} async-done(((f32[128,512]{1,0:T(8,128)}), f32[128,512]{1,0:T(8,128)}) %all-reduce.6.cloned.1.call-update) | async-done | bytes 262160 | tf_op jit(solution)/shard_map/psum | solution.py:80
  846.7 1.1 multiply_reduce_fusion
  847.8 1.0 fusion.8
  848.8 1.8 convolution_bitcast_fusion
  851.2 1087.0 %all-reduce.8.cloned.1.call-done = f32[2048,256]{0,1:T(8,128)} async-done(((f32[2048,256]{0,1:T(8,128)}), f32[2048,256]{0,1:T(8,128)}) %all-reduce.8.cloned.1.call-update) | async-done | bytes 2097168 | tf_op jit(solution)/shard_map/psum | solution.py:93
  1938.2 2.9 copy.7
  (15 shorter events, 0.2 us)
Async XLA Ops:
  7.2 1.2 copy-start
  7.2 233.6 %all-gather.2.cloned.1.call-start = ((), (), s32[]{:S(2)}) async-start(), calls=%async_computation | async-start | bytes 8454144 | tf_op jit(solution)/shard_map/all_gather | solution.py:44
  16.5 830.2 %all-reduce.6.cloned.1.call-start = ((), (), s32[]{:S(2)}) async-start(), calls=%async_computation.1 | async-start | bytes 524288 | tf_op jit(solution)/shard_map/psum | solution.py:80
  799.8 49.0 %copy-start.1 = (bf16[128,2048]{1,0:T(8,128)(2,1)S(1)}, bf16[128,2048]{1,0:T(8,128)(2,1)}, u32[]{:S(2)}) copy-start(bf16[128,2048]{1,0:T(8,128)(2,1)} %param.3) | copy-start | bytes 1572868
  807.4 1130.8 %all-reduce.8.cloned.1.call-start = ((), (), s32[]{:S(2)}) async-start(), calls=%async_computation.2 | async-start | bytes 4194304 | tf_op jit(solution)/shard_map/psum | solution.py:93
  848.8 1092.3 %copy-start.2 = (f32[128,256]{1,0:T(8,128)}, f32[128,256]{1,0:T(8,128)S(1)}, u32[]{:S(2)}) copy-start(f32[128,256]{1,0:T(8,128)S(1)} %fusion.8) | copy-start | bytes 393220
Sparse Core Ops, SparseCore 0:
  16.6 224.0 all-gather.1
  807.5 39.1 all-reduce.5
  850.7 1087.4 all-reduce.7
where the time goes:
time: 1950 us
  waiting for transfers between devices  1350 us (69%)
  blocking collectives  556 us (29%)
    psum x1, waiting for transfers between devices, per_device(): lax.psum((weight_part, jnp.sum(sample_cost_vector)), 'dp')  1090 us
    psum x1, blocking collectives, per_device(): lax.psum((weight_part, jnp.sum(sample_cost_vector)), 'dp')  545 us
    all_gather x1, waiting for transfers between devices, per_device(): block = lax.all_gather(own_half, 'dp', axis=0, tiled=True)  220 us
    psum x1, waiting for transfers between devices, per_device(): lax.psum(incomplete_derivative, 'mp')  39.2 us
  transfers between devices with their start and end apart: 3, of which 3 were waited for; matrix products, arithmetic and copies ran while one was open for 0% of the time, Pallas kernels for 0%

commit v1 on v0

v1 whole, which is shorter than its diff:
```python
import jax
import jax.numpy as jnp
from jax import lax
from jax.experimental import pallas as pl
from jax.experimental.pallas import tpu as pltpu
from jax.sharding import PartitionSpec as P

MESH = pl.DeviceIdType.MESH
F32 = jnp.float32
BF16 = jnp.bfloat16
SHARPNESS = 10.0
R = 128
NZ, NY, NX, NC = 8, 4, 2, 2
ROWS = R * NZ * NY * NX * NC

PLANE = [(ky, kx, kh) for ky in range(NY) for kx in range(2) for kh in range(2)]
COLUMN = [(kz, kc) for kz in range(NZ) for kc in range(2)]
GROUP = [(kx, kc) for kx in range(2) for kc in range(2)]


def nt(a, b):
    return lax.dot_general(a, b, (((1,), (1,)), ((), ())), preferred_element_type=F32)


def to_rows(x):
    return jnp.sum(x.T, axis=0, keepdims=True)


def to_columns(row):
    return jnp.broadcast_to(row, (R, R)).T


def kernel(
    h_ref, w_ref, perm_ref,
    loss_ref, gemb_ref, gproj_ref,
    ui, uj, raw, sim, mark, rowmsg, colmsg, losses, tsum,
    gs, gr, gpart, g4, hq, gp, gpb, ry, rz, rzb,
    s_mp, r_mp, s_i, r_i, s_j, r_j, s_f, r_f, s_row, r_row, s_col, r_col,
    s_loss, r_loss, s_rs, r_rs, s_h, r_h, s_g, r_g, s_y, r_y, s_z, r_z,
    s_az, r_az, s_ay, r_ay, s_ax, r_ax, s_ac, r_ac,
):
    dp = lax.axis_index("dp")
    xh = lax.axis_index("mp")
    c = lax.rem(dp, 2)
    xl = lax.rem(dp // 2, 2)
    y = lax.rem(dp // 4, 4)
    z = dp // 16
    p_me = y * 2 + xl
    q_me = xl * 2 + c

    def dev(z_, y_, xl_, c_, xh_):
        return (((z_ * 4 + y_) * 2 + xl_) * 2 + c_, xh_)

    def step(v, k, n):
        return v if k == 0 else lax.rem(v + k, n)

    def plane_dev(k):
        return dev(z, step(y, k[0], 4), step(xl, k[1], 2), c, step(xh, k[2], 2))

    def column_dev(k):
        return dev(step(z, k[0], 8), y, xl, step(c, k[1], 2), xh)

    def group_dev(k):
        return dev(z, y, step(xl, k[0], 2), step(c, k[1], 2), xh)

    me = (dp, xh)

    def send(src, dst, ssem, rsem, to):
        copy = pltpu.make_async_remote_copy(
            src_ref=src, dst_ref=dst, send_sem=ssem, recv_sem=rsem, device_id=to, device_id_type=MESH
        )
        copy.start()
        return copy

    def arrived(dst, ssem, rsem, frm):
        pltpu.make_async_remote_copy(
            src_ref=dst, dst_ref=dst, send_sem=ssem, recv_sem=rsem, device_id=frm, device_id_type=MESH
        ).wait_recv()

    sent = []

    barrier = pltpu.get_barrier_semaphore()
    peers = [plane_dev(k) for k in PLANE[1:]] + [column_dev(k) for k in COLUMN[1:]] + [group_dev((1, 1))]
    for peer in peers:
        pl.semaphore_signal(barrier, inc=1, device_id=peer, device_id_type=MESH)

    embed = jnp.dot(h_ref[...], w_ref[...], preferred_element_type=F32).astype(BF16)
    raw[0] = embed
    pl.semaphore_wait(barrier, len(peers))
    partner_dev = plane_dev((0, 0, 1))
    sent.append(send(raw.at[0], raw.at[1], s_mp, r_mp, partner_dev))

    first = z < 4
    lanes = lax.broadcasted_iota(jnp.int32, (1, R), 1)
    b_row = []
    for zz in range(8):
        jglob = (((zz * 4 + y) * 2 + xl) * 2 + xh) * R + lanes
        if zz < 4:
            other = perm_ref[pl.ds(zz * 16 + y * 4 + xl * 2 + xh, 1), :] + ROWS // 2
        else:
            other = jnp.full((1, R), -1, jnp.int32)
        b_row.append(jnp.where(first, jglob, other).astype(F32))
    b_row = jnp.concatenate(b_row, axis=1)
    for p in range(8):
        mine = (z * 16 + p * 2 + c) * R + lanes
        pair = perm_ref[pl.ds(lax.rem(z, 4) * 16 + p * 2 + c, 1), :] + ROWS // 2
        a_row = jnp.where(first, pair, mine).astype(F32)
        a_col = to_columns(a_row)
        mark[p * R:(p + 1) * R, :] = jnp.where(
            jnp.concatenate([a_col] * 8, axis=1) == b_row, -2.0, 0.0
        )

    arrived(raw.at[1], s_mp, r_mp, partner_dev)
    e0 = raw[0].astype(F32)
    e1 = raw[1].astype(F32)
    inv = lax.rsqrt(jnp.sum(e0 * e0 + e1 * e1, axis=1, keepdims=True) + 1e-06)
    own_i = pl.ds(pl.multiple_of(p_me * R, R), R)
    own_j = pl.ds(pl.multiple_of(z * R, R), R)
    ui[0, own_i, :] = (e0 * inv).astype(BF16)
    ui[1, own_i, :] = (e1 * inv).astype(BF16)

    mine = ui.at[:, own_i, :]
    i_peers = [(ky, kx, 0) for ky in range(4) for kx in range(2)][1:]
    for n, k in enumerate(i_peers):
        sent.append(send(mine, mine, s_i.at[n], r_i.at[n], plane_dev(k)))

    @pl.when(c == xh)
    def _():
        uj[0, own_j, :] = ui[0, own_i, :]
        uj[1, own_j, :] = ui[1, own_i, :]
        here = uj.at[:, own_j, :]
        out = []
        for kz in range(1, 8):
            out.append(send(here, here, s_j.at[kz], r_j.at[kz], column_dev((kz, 0))))
        out.append(send(here, here, s_f.at[0], r_f.at[0], column_dev((0, 1))))
        for kz in range(1, 8):
            frm = lax.rem(z + (8 - kz), 8)
            part = uj.at[:, pl.ds(pl.multiple_of(frm * R, R), R), :]
            arrived(part, s_j.at[kz], r_j.at[kz], column_dev((8 - kz, 0)))
            out.append(send(part, part, s_f.at[kz], r_f.at[kz], column_dev((0, 1))))
        for copy in out:
            copy.wait_send()

    @pl.when(c != xh)
    def _():
        for kz in range(8):
            frm = lax.rem(z + (8 - kz), 8)
            part = uj.at[:, pl.ds(pl.multiple_of(frm * R, R), R), :]
            arrived(part, s_f.at[kz], r_f.at[kz], column_dev((0, 1)))

    for n, (ky, kx, _) in enumerate(i_peers):
        frm = lax.rem(y + (4 - ky), 4) * 2 + lax.rem(xl + (2 - kx), 2)
        part = ui.at[:, pl.ds(pl.multiple_of(frm * R, R), R), :]
        arrived(part, s_i.at[n], r_i.at[n], plane_dev(((4 - ky) % 4, (2 - kx) % 2, 0)))

    for n, k in enumerate(GROUP):
        q = step(xl, k[0], 2) * 2 + step(c, k[1], 2)
        cols = pl.ds(pl.multiple_of(q * 512, 512), 512)
        if n == 0:
            hq[0:R, :] = h_ref[:, cols]
        else:
            sent.append(
                send(h_ref.at[:, cols], hq.at[n * R:(n + 1) * R, :], s_h.at[n], r_h.at[n], group_dev(k))
            )

    for b in range(4):
        rows = slice(b * 256, (b + 1) * 256)
        sim[rows, :] = nt(ui[0, rows, :], uj[0]) + nt(ui[1, rows, :], uj[1])
    eye = lax.broadcasted_iota(jnp.int32, (R, R), 0) == lax.broadcasted_iota(jnp.int32, (R, R), 1)
    block = sim[own_i, own_j]
    sim[own_i, own_j] = jnp.where(jnp.logical_and(eye, c == xh), -1e9, block)

    own_row = p_me * 2 + xh
    own_col = z * 2 + c
    tsum[...] = jnp.zeros_like(tsum)
    rowmsg[own_row] = jnp.zeros((16, R), F32)

    @pl.loop(0, 8)
    def _(p):
        rows = pl.ds(pl.multiple_of(p * R, R), R)
        s = sim[rows, :]
        hit = s * mark[rows, :]
        e = jnp.exp(SHARPNESS * (s - 1.0))
        sim[rows, :] = e
        part = e[:, 0:R]
        hits = hit[:, 0:R]
        for t in range(1, 8):
            part = part + e[:, t * R:(t + 1) * R]
            hits = hits + hit[:, t * R:(t + 1) * R]
        rowmsg[own_row, pl.ds(p, 1), :] = to_rows(part)
        rowmsg[own_row, 8:9, :] = rowmsg[own_row, 8:9, :] - 0.5 * jnp.sum(hits, axis=0, keepdims=True)
        tsum[...] = tsum[...] + jnp.sum(e, axis=0, keepdims=True)

    total = tsum[...]
    for zz in range(8):
        colmsg[own_col, zz:zz + 1, :] = total[:, zz * R:(zz + 1) * R]

    for n, k in enumerate(PLANE):
        if n:
            there = rowmsg.at[own_row]
            sent.append(send(there, there, s_row.at[n], r_row.at[n], plane_dev(k)))
    for n, k in enumerate(COLUMN):
        if n:
            there = colmsg.at[own_col]
            sent.append(send(there, there, s_col.at[n], r_col.at[n], column_dev(k)))
    for n, k in enumerate(PLANE):
        if n:
            back = ((4 - k[0]) % 4, k[1], k[2])
            frm = (step(y, back[0], 4) * 2 + step(xl, back[1], 2)) * 2 + step(xh, back[2], 2)
            arrived(rowmsg.at[frm], s_row.at[n], r_row.at[n], plane_dev(back))
    for n, k in enumerate(COLUMN):
        if n:
            back = ((8 - k[0]) % 8, k[1])
            frm = step(z, back[0], 8) * 2 + step(c, back[1], 2)
            arrived(colmsg.at[frm], s_col.at[n], r_col.at[n], column_dev(back))

    all_rows = rowmsg[0]
    all_cols = colmsg[0]
    for n in range(1, 16):
        all_rows = all_rows + rowmsg[n]
        all_cols = all_cols + colmsg[n]
    row_total = all_rows[0:8]
    hit_total = all_rows[8:9]

    cost = jnp.sum(jnp.log(row_total), axis=0, keepdims=True) - SHARPNESS * (hit_total - 8.0)
    losses[own_col] = jnp.broadcast_to(cost, (8, R))
    for n, k in enumerate(COLUMN):
        if n:
            there = losses.at[own_col]
            sent.append(send(there, there, s_loss.at[n], r_loss.at[n], column_dev(k)))

    inv_rows = 1.0 / row_total
    inv_cols = 1.0 / all_cols
    tsum[...] = jnp.concatenate([inv_cols[t:t + 1] for t in range(8)], axis=1)
    losses_t = gpart
    for p in range(8):
        losses_t[p] = to_columns(inv_rows[p:p + 1])
    for ky in range(4):
        y_to = step(y, ky, 4)
        rows = pl.ds(pl.multiple_of(y_to * 256, 256), 256)
        col = losses_t[pl.ds(y_to * 2, 2)].reshape(256, R)
        wide = jnp.concatenate([col] * 8, axis=1)
        weights = (sim[rows, :] * (wide + tsum[...]) + mark[rows, :]).astype(BF16)
        acc = None
        for f in range(2):
            g = jnp.dot(weights, uj[f], preferred_element_type=F32)
            gs[ky, 0, f, 0:R, :] = g[0:R].astype(BF16)
            gs[ky, 1, f, 0:R, :] = g[R:].astype(BF16)
            t = g * ui[f, rows, :].astype(F32)
            t = t[:, 0:R] + t[:, R:]
            acc = t if acc is None else acc + t
        for half in range(2):
            v = to_rows(acc[half * R:(half + 1) * R])
            hi = v.astype(BF16)
            lo = (v - hi.astype(F32)).astype(BF16)
            line = jnp.broadcast_to(jnp.concatenate([hi, lo], axis=1).astype(F32), (16, 256)).astype(BF16)
            gs[ky, half, 0, R:, :] = line
            gs[ky, half, 1, R:, :] = line
        for kx in range(2):
            for kh in range(2):
                n = (ky * 2 + kx) * 2 + kh
                if n:
                    sent.append(
                        send(
                            gs.at[ky, step(xl, kx, 2), kh], gr.at[n], s_rs.at[n], r_rs.at[n],
                            plane_dev((ky, kx, kh)),
                        )
                    )
    g = gs[0, xl, 0].astype(F32)
    for n, k in enumerate(PLANE):
        if n:
            arrived(gr.at[n], s_rs.at[n], r_rs.at[n], plane_dev(((4 - k[0]) % 4, k[1], k[2])))
            g = g + gr[n].astype(F32)
    inner = to_columns(g[R:R + 1, 0:R] + g[R:R + 1, R:])
    unit = raw[0].astype(F32) * inv
    grad = (SHARPNESS * inv) * (g[0:R] - unit * jnp.concatenate([inner, inner], axis=1))
    gemb_ref[...] = grad
    g4[0:R, :] = grad.astype(BF16)

    for n, k in enumerate(GROUP):
        if n:
            sent.append(
                send(g4.at[0:R, :], g4.at[n * R:(n + 1) * R, :], s_g.at[n], r_g.at[n], group_dev(k))
            )
    for n, k in enumerate(GROUP):
        if n:
            arrived(hq.at[n * R:(n + 1) * R, :], s_h.at[n], r_h.at[n], group_dev(k))
            arrived(g4.at[n * R:(n + 1) * R, :], s_g.at[n], r_g.at[n], group_dev(k))
    full = lax.dot_general(hq[...], g4[...], (((0,), (0,)), ((), ())), preferred_element_type=F32)
    gp[...] = full
    gpb[...] = full.astype(BF16)
    for ky in range(1, 4):
        y_to = step(y, ky, 4)
        part = gpb.at[pl.ds(pl.multiple_of(y_to * R, R), R), :]
        sent.append(send(part, ry.at[ky], s_y.at[ky], r_y.at[ky], plane_dev((ky, 0, 0))))
    part = gp[pl.ds(pl.multiple_of(y * R, R), R), :]
    for ky in range(1, 4):
        arrived(ry.at[ky], s_y.at[ky], r_y.at[ky], plane_dev((4 - ky, 0, 0)))
        part = part + ry[ky].astype(F32)
    gp[0:R, :] = part
    rzb[...] = part.astype(BF16)
    for kz in range(1, 8):
        z_to = step(z, kz, 8)
        piece = rzb.at[pl.ds(pl.multiple_of(z_to * 16, 16), 16), :]
        sent.append(send(piece, rz.at[kz], s_z.at[kz], r_z.at[kz], column_dev((kz, 0))))
    piece = gp[pl.ds(pl.multiple_of(z * 16, 16), 16), :]
    for kz in range(1, 8):
        arrived(rz.at[kz], s_z.at[kz], r_z.at[kz], column_dev((8 - kz, 0)))
        piece = piece + rz[kz].astype(F32)

    def span(q_, y_, z_):
        return pl.ds(pl.multiple_of(q_ * 512 + y_ * R + z_ * 16, 16), 16)

    gproj_ref[span(q_me, y, z), :] = piece.astype(BF16)
    there = gproj_ref.at[span(q_me, y, z), :]
    for kz in range(1, 8):
        sent.append(send(there, there, s_az.at[kz], r_az.at[kz], column_dev((kz, 0))))
    for kz in range(1, 8):
        frm = gproj_ref.at[span(q_me, y, step(z, 8 - kz, 8)), :]
        arrived(frm, s_az.at[kz], r_az.at[kz], column_dev((8 - kz, 0)))
    there = gproj_ref.at[pl.ds(pl.multiple_of(q_me * 512 + y * R, R), R), :]
    for ky in range(1, 4):
        sent.append(send(there, there, s_ay.at[ky], r_ay.at[ky], plane_dev((ky, 0, 0))))
    for ky in range(1, 4):
        y_from = step(y, 4 - ky, 4)
        frm = gproj_ref.at[pl.ds(pl.multiple_of(q_me * 512 + y_from * R, R), R), :]
        arrived(frm, s_ay.at[ky], r_ay.at[ky], plane_dev((4 - ky, 0, 0)))

    def quarter(q):
        return gproj_ref.at[pl.ds(pl.multiple_of(q * 512, 512), 512), :]

    there = quarter(q_me)
    sent.append(send(there, there, s_ax, r_ax, group_dev((1, 0))))
    sent.append(send(there, there, s_ac.at[0], r_ac.at[0], group_dev((0, 1))))
    there = quarter((1 - xl) * 2 + c)
    arrived(there, s_ax, r_ax, group_dev((1, 0)))
    sent.append(send(there, there, s_ac.at[1], r_ac.at[1], group_dev((0, 1))))

    for n, k in enumerate(COLUMN):
        if n:
            back = ((8 - k[0]) % 8, k[1])
            frm = step(z, back[0], 8) * 2 + step(c, back[1], 2)
            arrived(losses.at[frm], s_loss.at[n], r_loss.at[n], column_dev(back))
    cost = losses[0]
    for n in range(1, 16):
        cost = cost + losses[n]
    loss_ref[...] = jnp.broadcast_to(jnp.sum(cost, axis=1, keepdims=True) * (1.0 / ROWS), (8, R))

    arrived(quarter(xl * 2 + (1 - c)), s_ac.at[0], r_ac.at[0], group_dev((0, 1)))
    arrived(quarter((1 - xl) * 2 + (1 - c)), s_ac.at[1], r_ac.at[1], group_dev((0, 1)))
    for copy in sent:
        copy.wait_send()


def per_device(head_hidden, proj_weight, pair_perm):
    dma = pltpu.SemaphoreType.DMA
    vmem = pltpu.VMEM
    space = pl.BlockSpec(memory_space=pltpu.VMEM)
    pairs = []
    for shape in [(), (7,), (8,), (8,), (16,), (16,), (16,), (16,), (4,), (4,), (4,), (8,), (8,), (4,), (), (2,)]:
        pairs += [dma(shape), dma(shape)]
    loss, grad_emb, grad_proj = pl.pallas_call(
        kernel,
        out_shape=(
            jax.ShapeDtypeStruct((8, R), F32),
            jax.ShapeDtypeStruct((R, 256), F32),
            jax.ShapeDtypeStruct((2048, 256), BF16),
        ),
        in_specs=[space] * 3,
        out_specs=[space] * 3,
        scratch_shapes=[
            vmem((2, 1024, 256), BF16),
            vmem((2, 1024, 256), BF16),
            vmem((2, R, 256), BF16),
            vmem((1024, 1024), F32),
            vmem((1024, 1024), F32),
            vmem((16, 16, R), F32),
            vmem((16, 8, R), F32),
            vmem((16, 8, R), F32),
            vmem((1, 1024), F32),
            vmem((4, 2, 2, R + 16, 256), BF16),
            vmem((16, R + 16, 256), BF16),
            vmem((8, R, R), F32),
            vmem((512, 256), BF16),
            vmem((512, 512), BF16),
            vmem((512, 256), F32),
            vmem((512, 256), BF16),
            vmem((4, R, 256), BF16),
            vmem((8, 16, 256), BF16),
            vmem((R, 256), BF16),
        ] + pairs,
        compiler_params=pltpu.CompilerParams(
            collective_id=0, has_side_effects=True, vmem_limit_bytes=48 * 1024 * 1024
        ),
    )(head_hidden, proj_weight, pair_perm.reshape(64, R))
    return loss[0, 0], grad_emb, grad_proj.astype(F32)


def solution(mesh):
    placed = (P("dp", None), P(None, "mp"), P())
    return jax.shard_map(
        per_device,
        mesh=mesh,
        in_specs=placed,
        out_specs=(P(), P("dp", "mp"), P(None, "mp")),
        check_vma=False,
    )
```

time: 1950 us -> 101 us (0.05)
  waiting for transfers between devices: 1350 us -> 0 us
  blocking collectives: 556 us -> 0 us
  Pallas kernels: 0 us -> 94 us
    psum x2 -> x0, waiting for transfers between devices: 1130 us -> none  [the longest x1 1090 us: per_device(): lax.psum((weight_part, jnp.sum(sample_cost_vector)), 'dp')]
    psum x2 -> x0, blocking collectives: 550 us -> none  [the longest x1 545 us: per_device(): lax.psum((weight_part, jnp.sum(sample_cost_vector)), 'dp')]
    all_gather x1 -> x0, waiting for transfers between devices: 220 us -> none  [per_device(): block = lax.all_gather(own_half, 'dp', axis=0, tiled=True)]
    pallas_call x0 -> x1, Pallas kernels: none -> 94 us  [per_device(): pl.pallas_call(kernel, out_shape=(jax.ShapeDtypeStruct((8, R), F32), jax....]
  transfers between devices with their start and end apart: 3 -> 0, of which waited for: 3 -> 0; matrix products, arithmetic and copies ran while one was open for 0% -> 0% of each run, Pallas kernels for 0% -> 0%
where the time goes in v1:
time: 101 us; the launch traced here: 100 us
  Pallas kernels  94 us (93%)
  local copies, waits for them, and re-layouts  4.18 us (4%)
  other arithmetic  1.48 us (1%)
    pallas_call x1, Pallas kernels, per_device(): pl.pallas_call(kernel, out_shape=(jax.ShapeDtypeStruct((8, R), F32), jax....  94 us
    unnamed x7, local copies, waits for them, and re-layouts  3.67 us

profile of v1, /device:TPU:1, one launch (start us, length us, event | category | flops | bytes accessed | tf_op | source)
XLA Modules:
  0.0 100.3 jit_solution(3684306701559227485)
XLA Ops:
  0.6 0.0 copy-start
  0.6 1.2 %copy-done = bf16[2048,256]{1,0:T(8,128)(2,1)S(1)} copy-done((bf16[2048,256]{1,0:T(8,128)(2,1)S(1)}, bf16[2048,256]{1,0:T(8,128)(2,1)}, u32[]{:S(2)}) %copy-start) | copy-done | bytes 1048600
  1.9 0.0 copy-start.1
  1.9 1.0 %copy-done.1 = bf16[128,2048]{1,0:T(8,128)(2,1)S(1)} copy-done((bf16[128,2048]{1,0:T(8,128)(2,1)S(1)}, bf16[128,2048]{1,0:T(8,128)(2,1)}, u32[]{:S(2)}) %copy-start.1) | copy-done | bytes 524312
  2.9 0.0 copy-start.2
  2.9 0.8 copy-done.2
  3.7 94.0 %shard_map.58 = (f32[8,128]{1,0:T(8,128)S(1)}, f32[128,256]{1,0:T(8,128)S(1)}, bf16[2048,256]{1,0:T(8,128)(2,1)S(1)}) custom-call(bf16[128,2048]{1,0:T(8,128)(2,1)S(1)} %copy-done.1, bf16[2048,256]{1,0:T(8,128)(2,1)S(1)} %copy-done, s32[64,128]{1,0:T(8,128)S(1)} %bitcast.2), custom_call_target="tpu_custom_call" | custom-call | tf_op jit(solution)/shard_map/pallas_call | solution.py:362
  97.7 0.5 slice.3
  98.2 1.5 %convert_element_type.3 = f32[2048,256]{1,0:T(8,128)} convert(bf16[2048,256]{1,0:T(8,128)(2,1)S(1)} %get-tuple-element.8) | non-fusion elementwise | flops 524288 | bytes 3145728 | tf_op jit(solution)/shard_map/convert_element_type | solution.py:396
  99.7 0.7 copy.7
Async XLA Ops:
  0.6 1.2 %copy-start = (bf16[2048,256]{1,0:T(8,128)(2,1)S(1)}, bf16[2048,256]{1,0:T(8,128)(2,1)}, u32[]{:S(2)}) copy-start(bf16[2048,256]{1,0:T(8,128)(2,1)} %w_ref.1) | copy-start | bytes 3145732
  1.9 1.0 %copy-start.1 = (bf16[128,2048]{1,0:T(8,128)(2,1)S(1)}, bf16[128,2048]{1,0:T(8,128)(2,1)}, u32[]{:S(2)}) copy-start(bf16[128,2048]{1,0:T(8,128)(2,1)} %h_ref.1) | copy-start | bytes 1572868
  2.9 0.8 copy-start.2

commit v2 on v1

v2 whole, which is shorter than its diff:
```python
import jax
import jax.numpy as jnp
from jax import lax
from jax.experimental import pallas as pl
from jax.experimental.pallas import tpu as pltpu
from jax.sharding import PartitionSpec as P

MESH = pl.DeviceIdType.MESH
F32 = jnp.float32
BF16 = jnp.bfloat16
SHARPNESS = 10.0
R = 128
H = 64
ROWS = 16384
COPIES = 192


def far(k, n):
    return min(k, n - k)


PLANE = sorted([(ky, kx) for ky in range(4) for kx in range(4)][1:], key=lambda k: -far(k[0], 4) - far(k[1], 4))
COLUMN = sorted([(kz, kc) for kz in range(8) for kc in range(2)][1:], key=lambda k: -far(k[0], 8))
GROUP = [(kx, kc) for kx in range(2) for kc in range(2)]


def nt(a, b):
    return lax.dot_general(a, b, (((1,), (1,)), ((), ())), preferred_element_type=F32)


def to_rows(x):
    return jnp.sum(x.T, axis=0, keepdims=True)


def to_columns(row):
    return jnp.broadcast_to(row, (R, R)).T


def inverse_norm(e0, e1):
    return lax.rsqrt(jnp.sum(e0 * e0 + e1 * e1, axis=1, keepdims=True) + 1e-06)


def kernel(
    h_hbm, w_hbm, perm_hbm,
    loss_ref, gemb_ref, gproj_ref,
    h_ref, w_ref, perm_ref, ei, ej, ui, uj, sim, mark, rowmsg, colmsg, losses, tsum, factor,
    sa, sb, ra, rb, sa2, sb2, ra2, rb2, ia, ib, iar, ibr, ia2, ib2, iar2, ibr2, isum,
    g4, hq, gp, gpb, ry, rz, rzb, s_in, s_out, s_back,
):
    dp = lax.axis_index("dp")
    xh = lax.axis_index("mp")
    c = lax.rem(dp, 2)
    xl = lax.rem(dp // 2, 2)
    y = lax.rem(dp // 4, 4)
    z = dp // 16
    x = xh * 2 + xl
    p_me = y * 2 + xl
    q_me = xl * 2 + c
    fetches = c == xh

    def dev(dz=0, dy=0, dx=0, dc=0):
        x_ = step(x, dx, 4)
        return (((step(z, dz, 8) * 4 + step(y, dy, 4)) * 2 + lax.rem(x_, 2)) * 2 + step(c, dc, 2), x_ // 2)

    def step(v, k, n):
        k = k % n
        return v if k == 0 else lax.rem(v + k, n)

    def group_dev(kx, kc):
        return (((z * 4 + y) * 2 + step(xl, kx, 2)) * 2 + step(c, kc, 2), xh)

    slots = {}

    def copy(key, src, dst, to):
        n = slots.setdefault(key, len(slots))
        return pltpu.make_async_remote_copy(
            src_ref=src, dst_ref=dst, send_sem=s_out.at[n], recv_sem=s_back.at[n],
            device_id=to, device_id_type=MESH,
        )

    sent = []

    def send(key, src, dst, to):
        one = copy(key, src, dst, to)
        one.start()
        sent.append(one)

    def arrived(key, dst):
        copy(key, dst, dst, dev(dc=1)).wait_recv()

    loads = [
        pltpu.make_async_copy(h_hbm, h_ref, s_in.at[0]),
        pltpu.make_async_copy(w_hbm, w_ref, s_in.at[1]),
        pltpu.make_async_copy(perm_hbm, perm_ref, s_in.at[2]),
    ]
    for load in loads:
        load.start()

    barrier = pltpu.get_barrier_semaphore()
    peers = [dev(dz=kz, dc=kc) for kz, kc in COLUMN] + [dev(dy=ky, dx=kx) for ky, kx in PLANE] + [group_dev(1, 1)]
    for peer in peers:
        pl.semaphore_signal(barrier, inc=1, device_id=peer, device_id_type=MESH)
    for load in loads:
        load.wait()

    embed = jnp.dot(h_ref[...], w_ref[...], preferred_element_type=F32).astype(BF16)
    ei[y, x] = embed

    @pl.when(fetches)
    def _():
        ej[xh, z] = ei[y, x]

    pl.semaphore_wait(barrier, len(peers))

    own = ei.at[y, x]
    for k in (2, 1, 3):
        send(("x", k), own, own, dev(dx=k))
    for k in (1, 3, 2):
        send(("y", k), own, own, dev(dy=k))

    def along_z(half, f):
        piece = ej.at[f, z]
        for k in (2, 6, 1, 7):
            copy(("z", half, k), piece, piece, dev(dz=k)).start()
        copy(("c", half, 0), piece, piece, dev(dc=1)).start()

    @pl.when(fetches)
    def _():
        along_z(0, xh)

    first = z < 4
    lanes = lax.broadcasted_iota(jnp.int32, (1, R), 1)
    b_row = []
    for zz in range(8):
        jglob = (((zz * 4 + y) * 2 + xl) * 2 + xh) * R + lanes
        if zz < 4:
            other = perm_ref[pl.ds(zz * 16 + y * 4 + xl * 2 + xh, 1), :] + ROWS // 2
        else:
            other = jnp.full((1, R), -1, jnp.int32)
        b_row.append(jnp.where(first, jglob, other).astype(F32))
    b_row = jnp.concatenate(b_row, axis=1)
    for p in range(8):
        mine = (z * 16 + p * 2 + c) * R + lanes
        pair = perm_ref[pl.ds(lax.rem(z, 4) * 16 + p * 2 + c, 1), :] + ROWS // 2
        a_col = to_columns(jnp.where(first, pair, mine).astype(F32))
        mark[p * R:(p + 1) * R, :] = jnp.where(jnp.concatenate([a_col] * 8, axis=1) == b_row, -2.0, 0.0)

    def on_from_x(k):
        piece = ei.at[y, step(x, -k, 4)]
        arrived(("x", k), piece)
        part = ei.at[y, step(x, -k, 4), 0:H]
        for ky in (2, 1, 3):
            send(("xy", k, ky), part, part, dev(dy=ky))

    def on_from_y(k):
        piece = ei.at[step(y, -k, 4), x]
        arrived(("y", k), piece)
        part = ei.at[step(y, -k, 4), x, H:R]
        for kx in (2, 1, 3):
            send(("yx", k, kx), part, part, dev(dx=kx))

    on_from_x(1)
    on_from_x(3)
    on_from_y(1)
    on_from_y(3)
    on_from_x(2)

    @pl.when(fetches)
    def _():
        ej[1 - xh, z] = ei[y, step(x, 2, 4)]
        along_z(1, 1 - xh)

    on_from_y(2)

    def hand(half, f, k):
        piece = ej.at[f, step(z, -k, 8)]
        copy(("c", half, k), piece, piece, dev(dc=1)).start()

    def from_z(half, f, k):
        piece = ej.at[f, step(z, -k, 8)]
        if k == 4:
            for s in range(2):
                arrived(("z", half, 4, s), ej.at[f, step(z, 4, 8), s * H:(s + 1) * H])
        else:
            arrived(("z", half, k), piece)
        if k == 2:
            copy(("z", half, 3), piece, piece, dev(dz=1)).start()
            part = ej.at[f, step(z, -2, 8), 0:H]
            copy(("z", half, 4, 0), part, part, dev(dz=2)).start()
        if k == 6:
            copy(("z", half, 5), piece, piece, dev(dz=-1)).start()
            part = ej.at[f, step(z, 2, 8), H:R]
            copy(("z", half, 4, 1), part, part, dev(dz=-2)).start()
        hand(half, f, k)

    @pl.when(fetches)
    def _():
        for k in (2, 6, 1, 7):
            from_z(0, xh, k)
        for k in (2, 6, 1, 7):
            from_z(1, 1 - xh, k)

    for k in (1, 3, 2):
        for j in (1, 3, 2):
            arrived(("xy", k, j), ei.at[step(y, -j, 4), step(x, -k, 4), 0:H])
            arrived(("yx", k, j), ei.at[step(y, -k, 4), step(x, -j, 4), H:R])

    def unit(dst, rows, e0, e1):
        e0 = e0.astype(F32)
        e1 = e1.astype(F32)
        inv = inverse_norm(e0, e1)
        dst[0, rows, :] = (e0 * inv).astype(BF16)
        dst[1, rows, :] = (e1 * inv).astype(BF16)

    for p in range(8):
        unit(ui, slice(p * R, (p + 1) * R), ei[p // 2, p % 2], ei[p // 2, 2 + p % 2])

    @pl.when(fetches)
    def _():
        for half, f in ((0, xh), (1, 1 - xh)):
            for k in (3, 5, 4):
                from_z(half, f, k)

    @pl.when(jnp.logical_not(fetches))
    def _():
        for half, f in ((0, xh), (1, 1 - xh)):
            for k in range(8):
                arrived(("c", half, k), ej.at[f, step(z, -k, 8)])

    for zz in range(8):
        unit(uj, slice(zz * R, (zz + 1) * R), ej[0, zz], ej[1, zz])

    for n, (kx, kc) in enumerate(GROUP):
        q = step(xl, kx, 2) * 2 + step(c, kc, 2)
        quarter_columns = pl.ds(pl.multiple_of(q * 512, 512), 512)
        if n == 0:
            hq[0:R, :] = h_ref[:, quarter_columns]
        else:
            send(("h", n), h_ref.at[:, quarter_columns], hq.at[n * R:(n + 1) * R, :], group_dev(kx, kc))

    for b in range(4):
        rows = slice(b * 256, (b + 1) * 256)
        sim[rows, :] = nt(ui[0, rows, :], uj[0]) + nt(ui[1, rows, :], uj[1])
    own_i = pl.ds(pl.multiple_of(p_me * R, R), R)
    own_j = pl.ds(pl.multiple_of(z * R, R), R)
    eye = lax.broadcasted_iota(jnp.int32, (R, R), 0) == lax.broadcasted_iota(jnp.int32, (R, R), 1)
    block = sim[own_i, own_j]
    sim[own_i, own_j] = jnp.where(jnp.logical_and(eye, fetches), -1e9, block)

    own_row = y * 4 + x
    own_col = z * 2 + c
    tsum[...] = jnp.zeros_like(tsum)
    rowmsg[own_row] = jnp.zeros((16, R), F32)

    @pl.loop(0, 8)
    def _(p):
        rows = pl.ds(pl.multiple_of(p * R, R), R)
        s = sim[rows, :]
        hit = s * mark[rows, :]
        e = jnp.exp(SHARPNESS * (s - 1.0))
        sim[rows, :] = e
        part = e[:, 0:R]
        hits = hit[:, 0:R]
        for t in range(1, 8):
            part = part + e[:, t * R:(t + 1) * R]
            hits = hits + hit[:, t * R:(t + 1) * R]
        rowmsg[own_row, pl.ds(p, 1), :] = to_rows(part)
        rowmsg[own_row, 8:9, :] = rowmsg[own_row, 8:9, :] - 0.5 * jnp.sum(hits, axis=0, keepdims=True)
        tsum[...] = tsum[...] + jnp.sum(e, axis=0, keepdims=True)

    total = tsum[...]
    for zz in range(8):
        colmsg[own_col, zz:zz + 1, :] = total[:, zz * R:(zz + 1) * R]

    for kz, kc in COLUMN:
        send(("col", kz, kc), colmsg.at[own_col], colmsg.at[own_col], dev(dz=kz, dc=kc))
    for ky, kx in PLANE:
        send(("row", ky, kx), rowmsg.at[own_row], rowmsg.at[own_row], dev(dy=ky, dx=kx))
    for ky, kx in PLANE:
        arrived(("row", ky, kx), rowmsg.at[step(y, -ky, 4) * 4 + step(x, -kx, 4)])
    for kz, kc in COLUMN:
        arrived(("col", kz, kc), colmsg.at[step(z, -kz, 8) * 2 + step(c, kc, 2)])

    all_rows = rowmsg[0]
    all_cols = colmsg[0]
    for n in range(1, 16):
        all_rows = all_rows + rowmsg[n]
        all_cols = all_cols + colmsg[n]
    row_total = all_rows[0:8]
    hit_total = all_rows[8:9]
    cost = jnp.sum(jnp.log(row_total), axis=0, keepdims=True) - SHARPNESS * (hit_total - 8.0)
    losses[own_col] = jnp.broadcast_to(cost, (8, R))

    inv_rows = 1.0 / row_total
    inv_cols = 1.0 / all_cols
    tsum[...] = jnp.concatenate([inv_cols[t:t + 1] for t in range(8)], axis=1)
    for p in range(8):
        factor[p] = to_columns(inv_rows[p:p + 1])
    for ky in (2, 1, 3, 0):
        y_to = step(y, ky, 4)
        rows = pl.ds(pl.multiple_of(y_to * 256, 256), 256)
        wide = jnp.concatenate([factor[pl.ds(y_to * 2, 2)].reshape(256, R)] * 8, axis=1)
        weights = (sim[rows, :] * (wide + tsum[...]) + mark[rows, :]).astype(BF16)
        acc = None
        for f in range(2):
            g = jnp.dot(weights, uj[f], preferred_element_type=F32)
            for half in range(2):
                sa[2 * f + half, y_to] = g[half * R:half * R + H].astype(BF16)
                sb[y_to, 2 * f + half] = g[half * R + H:(half + 1) * R].astype(BF16)
            t = g * ui[f, rows, :].astype(F32)
            t = t[:, 0:R] + t[:, R:]
            acc = t if acc is None else acc + t
        for kx in (2, 1, 3):
            send(("ra", kx, ky), sa.at[step(x, kx, 4), y_to], ra.at[kx, y_to], dev(dx=kx))
        if ky:
            send(("rb", ky), sb.at[y_to], rb.at[ky], dev(dy=ky))
        for half in range(2):
            v = to_rows(acc[half * R:(half + 1) * R])
            ia[half, pl.ds(y_to, 1), :] = v
            ib[y_to, half:half + 1, :] = v
        if ky:
            send(("ib", ky), ib.at[y_to], ibr.at[ky], dev(dy=ky))
    for kx in (2, 1, 3):
        send(("ia", kx), ia.at[step(xl, kx, 2)], iar.at[kx], dev(dx=kx))
    for kz, kc in COLUMN:
        send(("loss", kz, kc), losses.at[own_col], losses.at[own_col], dev(dz=kz, dc=kc))

    for ky in (2, 1, 3):
        arrived(("rb", ky), rb.at[ky])
        arrived(("ib", ky), ibr.at[ky])
    line = ib[y] + ibr[1] + ibr[2] + ibr[3]
    isum[1] = line
    for half in range(2):
        ib2[half] = jnp.broadcast_to(line[half:half + 1], (8, R))
    for kx in (2, 1, 3):
        x_to = step(x, kx, 4)
        g = sb[y, x_to].astype(F32) + rb[1, x_to].astype(F32) + rb[2, x_to].astype(F32) + rb[3, x_to].astype(F32)
        sb2[kx] = g.astype(BF16)
        send(("rb2", kx), sb2.at[kx], rb2.at[kx], dev(dx=kx))
        send(("ib2", kx), ib2.at[step(xl, kx, 2)], ibr2.at[kx], dev(dx=kx))
    g_b = sb[y, x].astype(F32) + rb[1, x].astype(F32) + rb[2, x].astype(F32) + rb[3, x].astype(F32)
    for kx in (2, 1, 3):
        arrived(("ia", kx), iar.at[kx])
        for ky in range(4):
            arrived(("ra", kx, ky), ra.at[kx, step(y, ky, 4)])
    line = ia[xl] + iar[1] + iar[2] + iar[3]
    isum[0] = line
    for yy in range(4):
        ia2[yy] = jnp.broadcast_to(line[yy:yy + 1], (8, R))
    for ky in (2, 1, 3):
        y_to = step(y, ky, 4)
        g = sa[x, y_to].astype(F32) + ra[1, y_to].astype(F32) + ra[2, y_to].astype(F32) + ra[3, y_to].astype(F32)
        sa2[ky] = g.astype(BF16)
        send(("ra2", ky), sa2.at[ky], ra2.at[ky], dev(dy=ky))
        send(("ia2", ky), ia2.at[y_to], iar2.at[ky], dev(dy=ky))
    g_a = sa[x, y].astype(F32) + ra[1, y].astype(F32) + ra[2, y].astype(F32) + ra[3, y].astype(F32)
    inner_a = isum[0, pl.ds(y, 1), :]
    inner_b = isum[1, pl.ds(xl, 1), :]
    for k in (1, 3, 2):
        arrived(("rb2", k), rb2.at[k])
        arrived(("ib2", k), ibr2.at[k])
        arrived(("ra2", k), ra2.at[k])
        arrived(("ia2", k), iar2.at[k])
        g_a = g_a + ra2[k].astype(F32)
        g_b = g_b + rb2[k].astype(F32)
        inner_a = inner_a + iar2[k, 0:1]
        inner_b = inner_b + ibr2[k, 0:1]
    inner = to_columns(jnp.where(lanes < H, inner_a, inner_b))
    inv = inverse_norm(ei[y, xl].astype(F32), ei[y, 2 + xl].astype(F32))
    own_unit = ei[y, x].astype(F32) * inv
    g = jnp.concatenate([g_a, g_b], axis=0)
    grad = (SHARPNESS * inv) * (g - own_unit * jnp.concatenate([inner, inner], axis=1))
    gemb_ref[...] = grad
    g4[0:R, :] = grad.astype(BF16)

    for n, (kx, kc) in enumerate(GROUP):
        if n:
            send(("g", n), g4.at[0:R, :], g4.at[n * R:(n + 1) * R, :], group_dev(kx, kc))
    for n in range(1, 4):
        arrived(("h", n), hq.at[n * R:(n + 1) * R, :])
        arrived(("g", n), g4.at[n * R:(n + 1) * R, :])
    full = lax.dot_general(hq[...], g4[...], (((0,), (0,)), ((), ())), preferred_element_type=F32)
    gp[...] = full
    gpb[...] = full.astype(BF16)
    for ky in (2, 1, 3):
        part = gpb.at[pl.ds(pl.multiple_of(step(y, ky, 4) * R, R), R), :]
        send(("gy", ky), part, ry.at[ky], dev(dy=ky))
    part = gp[pl.ds(pl.multiple_of(y * R, R), R), :]
    for ky in (1, 3, 2):
        arrived(("gy", ky), ry.at[ky])
        part = part + ry[ky].astype(F32)
    gp[0:R, :] = part
    rzb[...] = part.astype(BF16)
    for kz in (4, 3, 5, 2, 6, 1, 7):
        piece = rzb.at[pl.ds(pl.multiple_of(step(z, kz, 8) * 16, 16), 16), :]
        send(("gz", kz), piece, rz.at[kz], dev(dz=kz))
    piece = gp[pl.ds(pl.multiple_of(z * 16, 16), 16), :]
    for kz in (1, 7, 2, 6, 3, 5, 4):
        arrived(("gz", kz), rz.at[kz])
        piece = piece + rz[kz].astype(F32)

    def rows_of(q_, y_, z_=None):
        if z_ is None:
            return gproj_ref.at[pl.ds(pl.multiple_of(q_ * 512 + y_ * R, R), R), :]
        return gproj_ref.at[pl.ds(pl.multiple_of(q_ * 512 + y_ * R + z_ * 16, 16), 16), :]

    gproj_ref[pl.ds(pl.multiple_of(q_me * 512 + y * R + z * 16, 16), 16), :] = piece.astype(BF16)
    mine = rows_of(q_me, y, z)
    for kz in (4, 3, 5, 2, 6, 1, 7):
        send(("az", kz), mine, mine, dev(dz=kz))
    for kz in (1, 7, 2, 6, 3, 5, 4):
        arrived(("az", kz), rows_of(q_me, y, step(z, -kz, 8)))

    def to_group(ky):
        there = rows_of(q_me, step(y, -ky, 4))
        send(("ax", ky), there, there, group_dev(1, 0))
        send(("ac", 0, ky), there, there, group_dev(0, 1))

    mine = rows_of(q_me, y)
    for ky in (2, 1, 3):
        send(("ay", ky), mine, mine, dev(dy=ky))
    to_group(0)
    for ky in (1, 3, 2):
        arrived(("ay", ky), rows_of(q_me, step(y, -ky, 4)))
        to_group(ky)
    for ky in (0, 1, 3, 2):
        there = rows_of((1 - xl) * 2 + c, step(y, -ky, 4))
        arrived(("ax", ky), there)
        send(("ac", 1, ky), there, there, group_dev(0, 1))

    for kz, kc in COLUMN:
        arrived(("loss", kz, kc), losses.at[step(z, -kz, 8) * 2 + step(c, kc, 2)])
    cost = losses[0]
    for n in range(1, 16):
        cost = cost + losses[n]
    loss_ref[...] = jnp.broadcast_to(jnp.sum(cost, axis=1, keepdims=True) * (1.0 / ROWS), (8, R))

    for ky in (0, 1, 3, 2):
        arrived(("ac", 0, ky), rows_of(xl * 2 + (1 - c), step(y, -ky, 4)))
        arrived(("ac", 1, ky), rows_of((1 - xl) * 2 + (1 - c), step(y, -ky, 4)))
    for one in sent:
        one.wait_send()

    @pl.when(fetches)
    def _():
        whole = ej.at[0, 0]
        half_piece = ej.at[0, 0, 0:H]
        for half in range(2):
            for k in (2, 6, 1, 7, 3, 5):
                copy(("z", half, k), whole, whole, dev(dc=1)).wait_send()
            for s in range(2):
                copy(("z", half, 4, s), half_piece, half_piece, dev(dc=1)).wait_send()
            for k in range(8):
                copy(("c", half, k), whole, whole, dev(dc=1)).wait_send()


def per_device(head_hidden, proj_weight, pair_perm):
    vmem = pltpu.VMEM
    hbm = pl.BlockSpec(memory_space=pltpu.HBM)
    space = pl.BlockSpec(memory_space=pltpu.VMEM)
    loss, grad_emb, grad_proj = pl.pallas_call(
        kernel,
        out_shape=(
            jax.ShapeDtypeStruct((8, R), F32),
            jax.ShapeDtypeStruct((R, 256), F32),
            jax.ShapeDtypeStruct((2048, 256), BF16),
        ),
        in_specs=[hbm] * 3,
        out_specs=[space] * 3,
        scratch_shapes=[
            vmem((R, 2048), BF16),
            vmem((2048, 256), BF16),
            vmem((64, R), jnp.int32),
            vmem((4, 4, R, 256), BF16),
            vmem((2, 8, R, 256), BF16),
            vmem((2, 1024, 256), BF16),
            vmem((2, 1024, 256), BF16),
            vmem((1024, 1024), F32),
            vmem((1024, 1024), F32),
            vmem((16, 16, R), F32),
            vmem((16, 8, R), F32),
            vmem((16, 8, R), F32),
            vmem((1, 1024), F32),
            vmem((8, R, R), F32),
            vmem((4, 4, H, 256), BF16),
            vmem((4, 4, H, 256), BF16),
            vmem((4, 4, H, 256), BF16),
            vmem((4, 4, H, 256), BF16),
            vmem((4, H, 256), BF16),
            vmem((4, H, 256), BF16),
            vmem((4, H, 256), BF16),
            vmem((4, H, 256), BF16),
            vmem((2, 8, R), F32),
            vmem((4, 8, R), F32),
            vmem((4, 8, R), F32),
            vmem((4, 8, R), F32),
            vmem((4, 8, R), F32),
            vmem((2, 8, R), F32),
            vmem((4, 8, R), F32),
            vmem((4, 8, R), F32),
            vmem((2, 8, R), F32),
            vmem((512, 256), BF16),
            vmem((512, 512), BF16),
            vmem((512, 256), F32),
            vmem((512, 256), BF16),
            vmem((4, R, 256), BF16),
            vmem((8, 16, 256), BF16),
            vmem((R, 256), BF16),
            pltpu.SemaphoreType.DMA((3,)),
            pltpu.SemaphoreType.DMA((COPIES,)),
            pltpu.SemaphoreType.DMA((COPIES,)),
        ],
        compiler_params=pltpu.CompilerParams(
            collective_id=0, has_side_effects=True, vmem_limit_bytes=56 * 1024 * 1024
        ),
    )(head_hidden, proj_weight, pair_perm.reshape(64, R))
    return loss[0, 0], grad_emb, grad_proj.astype(F32)


def solution(mesh):
    placed = (P("dp", None), P(None, "mp"), P())
    return jax.shard_map(
        per_device,
        mesh=mesh,
        in_specs=placed,
        out_specs=(P(), P("dp", "mp"), P(None, "mp")),
        check_vma=False,
    )
```

time: 101 us -> 89.3 us (0.88)
  Pallas kernels: 94 us -> 84 us
  local copies, waits for them, and re-layouts: 4.18 us -> 1.88 us
  other arithmetic: 1.48 us -> 2.7 us
    pallas_call x1, Pallas kernels: 94 us -> 84 us  [per_device(): pl.pallas_call(kernel, out_shape=(jax.ShapeDtypeStruct((8, R), F32), jax....]
    unnamed x7 -> x3, local copies, waits for them, and re-layouts: 3.67 us -> 0.66 us
    convert_element_type x1, other arithmetic: 1.48 us -> 2.7 us  [per_device(): return (loss[0, 0], grad_emb, grad_proj.astype(F32))]
where the time goes in v2:
time: 89.3 us; the launch traced here: 89.2 us
  Pallas kernels  84 us (94%)
  other arithmetic  2.7 us (3%)
  local copies, waits for them, and re-layouts  1.88 us (2%)
    pallas_call x1, Pallas kernels, per_device(): pl.pallas_call(kernel, out_shape=(jax.ShapeDtypeStruct((8, R), F32), jax....  84 us
    convert_element_type x1, other arithmetic, per_device(): return (loss[0, 0], grad_emb, grad_proj.astype(F32))  2.7 us

profile of v2, /device:TPU:1, one launch (start us, length us, event | category | flops | bytes accessed | tf_op | source)
XLA Modules:
  0.0 89.2 jit_solution(132798816970099674)
XLA Ops:
  0.6 84.0 %shard_map.58 = (f32[8,128]{1,0:T(8,128)}, f32[128,256]{1,0:T(8,128)}, bf16[2048,256]{1,0:T(8,128)(2,1)}) custom-call(bf16[128,2048]{1,0:T(8,128)(2,1)} %h_hbm.1, bf16[2048,256]{1,0:T(8,128)(2,1)} %w_hbm.1, s32[64,128]{1,0:T(8,128)} %bitcast.2), custom_call_target="tpu_custom_call" | custom-call | tf_op jit(solution)/shard_map/pallas_call | solution.py:461
  84.6 0.0 copy-start
  84.6 1.2 %slice.3 = f32[1,1]{1,0:T(1,128)} slice(f32[8,128]{1,0:T(8,128)} %get-tuple-element.6), slice={[0:1], [0:1]} | slice | bytes 8 | tf_op jit(solution)/shard_map/slice | solution.py:517
  85.8 2.7 %convert_element_type.3 = f32[2048,256]{1,0:T(8,128)} convert(bf16[2048,256]{1,0:T(8,128)(2,1)} %get-tuple-element.8) | non-fusion elementwise | flops 524288 | bytes 3145728 | tf_op jit(solution)/shard_map/convert_element_type | solution.py:517
  88.5 0.0 copy-done
  88.5 0.7 copy.7
Async XLA Ops:
  84.6 3.9 %copy-start = (f32[128,256]{1,0:T(8,128)S(1)}, f32[128,256]{1,0:T(8,128)}, u32[]{:S(2)}) copy-start(f32[128,256]{1,0:T(8,128)} %get-tuple-element.13) | copy-start | bytes 393220

commit v3 on v2

--- a/solution.py
+++ b/solution.py
@@ -9,10 +9,12 @@
 F32 = jnp.float32
 BF16 = jnp.bfloat16
 SHARPNESS = 10.0
+EXP2_SCALE = SHARPNESS * 1.4426950408889634
+ORDER = (0, 1, 7, 2, 6, 3, 5, 4)
 R = 128
 H = 64
 ROWS = 16384
-COPIES = 192
+COPIES = 224
 
 
 def far(k, n):
@@ -43,7 +45,7 @@
 def kernel(
     h_hbm, w_hbm, perm_hbm,
     loss_ref, gemb_ref, gproj_ref,
-    h_ref, w_ref, perm_ref, ei, ej, ui, uj, sim, mark, rowmsg, colmsg, losses, tsum, factor,
+    h_ref, w_ref, perm_ref, ei, ej, ui, uj, sim, mark, rowmsg, colmsg, losses, tsum, isum_cols, rowacc, factor,
     sa, sb, ra, rb, sa2, sb2, ra2, rb2, ia, ib, iar, ibr, ia2, ib2, iar2, ibr2, isum,
     g4, hq, gp, gpb, ry, rz, rzb, s_in, s_out, s_back,
 ):
@@ -131,13 +133,11 @@
     first = z < 4
     lanes = lax.broadcasted_iota(jnp.int32, (1, R), 1)
     b_row = []
-    for zz in range(8):
+    for k in ORDER:
+        zz = step(z, -k, 8)
         jglob = (((zz * 4 + y) * 2 + xl) * 2 + xh) * R + lanes
-        if zz < 4:
-            other = perm_ref[pl.ds(zz * 16 + y * 4 + xl * 2 + xh, 1), :] + ROWS // 2
-        else:
-            other = jnp.full((1, R), -1, jnp.int32)
-        b_row.append(jnp.where(first, jglob, other).astype(F32))
+        pair = perm_ref[pl.ds(lax.rem(zz, 4) * 16 + y * 4 + xl * 2 + xh, 1), :] + ROWS // 2
+        b_row.append(jnp.where(first, jglob, jnp.where(zz < 4, pair, -1)).astype(F32))
     b_row = jnp.concatenate(b_row, axis=1)
     for p in range(8):
         mine = (z * 16 + p * 2 + c) * R + lanes
@@ -215,22 +215,8 @@
     for p in range(8):
         unit(ui, slice(p * R, (p + 1) * R), ei[p // 2, p % 2], ei[p // 2, 2 + p % 2])
 
-    @pl.when(fetches)
-    def _():
-        for half, f in ((0, xh), (1, 1 - xh)):
-            for k in (3, 5, 4):
-                from_z(half, f, k)
-
-    @pl.when(jnp.logical_not(fetches))
-    def _():
-        for half, f in ((0, xh), (1, 1 - xh)):
-            for k in range(8):
-                arrived(("c", half, k), ej.at[f, step(z, -k, 8)])
-
-    for zz in range(8):
-        unit(uj, slice(zz * R, (zz + 1) * R), ej[0, zz], ej[1, zz])
-
-    for n, (kx, kc) in enumerate(GROUP):
+    def send_hidden(n):
+        kx, kc = GROUP[n]
         q = step(xl, kx, 2) * 2 + step(c, kc, 2)
         quarter_columns = pl.ds(pl.multiple_of(q * 512, 512), 512)
         if n == 0:
@@ -238,44 +224,75 @@
         else:
             send(("h", n), h_ref.at[:, quarter_columns], hq.at[n * R:(n + 1) * R, :], group_dev(kx, kc))
 
-    for b in range(4):
-        rows = slice(b * 256, (b + 1) * 256)
-        sim[rows, :] = nt(ui[0, rows, :], uj[0]) + nt(ui[1, rows, :], uj[1])
-    own_i = pl.ds(pl.multiple_of(p_me * R, R), R)
-    own_j = pl.ds(pl.multiple_of(z * R, R), R)
-    eye = lax.broadcasted_iota(jnp.int32, (R, R), 0) == lax.broadcasted_iota(jnp.int32, (R, R), 1)
-    block = sim[own_i, own_j]
-    sim[own_i, own_j] = jnp.where(jnp.logical_and(eye, fetches), -1e9, block)
+    for n in range(3):
+        send_hidden(n)
 
     own_row = y * 4 + x
     own_col = z * 2 + c
-    tsum[...] = jnp.zeros_like(tsum)
+    rowacc[...] = jnp.zeros_like(rowacc)
     rowmsg[own_row] = jnp.zeros((16, R), F32)
 
-    @pl.loop(0, 8)
-    def _(p):
-        rows = pl.ds(pl.multiple_of(p * R, R), R)
-        s = sim[rows, :]
-        hit = s * mark[rows, :]
-        e = jnp.exp(SHARPNESS * (s - 1.0))
-        sim[rows, :] = e
-        part = e[:, 0:R]
-        hits = hit[:, 0:R]
-        for t in range(1, 8):
-            part = part + e[:, t * R:(t + 1) * R]
-            hits = hits + hit[:, t * R:(t + 1) * R]
-        rowmsg[own_row, pl.ds(p, 1), :] = to_rows(part)
-        rowmsg[own_row, 8:9, :] = rowmsg[own_row, 8:9, :] - 0.5 * jnp.sum(hits, axis=0, keepdims=True)
-        tsum[...] = tsum[...] + jnp.sum(e, axis=0, keepdims=True)
-
-    total = tsum[...]
-    for zz in range(8):
-        colmsg[own_col, zz:zz + 1, :] = total[:, zz * R:(zz + 1) * R]
+    def columns(first_slot, last_slot):
+        for slot in range(first_slot, last_slot):
+            zz = step(z, -ORDER[slot], 8)
+            unit(uj, slice(slot * R, (slot + 1) * R), ej[0, zz], ej[1, zz])
+        cols = slice(first_slot * R, last_slot * R)
+        sums = None
+        hits = None
+        for b in range(4):
+            rows = slice(b * 256, (b + 1) * 256)
+            s = nt(ui[0, rows, :], uj[0, cols, :]) + nt(ui[1, rows, :], uj[1, cols, :])
+            hit = jnp.sum(s * mark[rows, cols], axis=0, keepdims=True)
+            e = jnp.exp2(EXP2_SCALE * s - EXP2_SCALE)
+            if first_slot == 0:
+                at = lax.broadcasted_iota(jnp.int32, (256, R), 0) - lax.broadcasted_iota(jnp.int32, (256, R), 1)
+                diagonal = at == jnp.where(fetches, p_me * R - b * 256, -ROWS)
+                e = jnp.concatenate([jnp.where(diagonal, 0.0, e[:, 0:R]), e[:, R:]], axis=1)
+            sim[rows, cols] = e
+            part = e[:, 0:R]
+            for t in range(1, last_slot - first_slot):
+                part = part + e[:, t * R:(t + 1) * R]
+            rowacc[rows, :] = rowacc[rows, :] + part
+            total = jnp.sum(e, axis=0, keepdims=True)
+            sums = total if sums is None else sums + total
+            hits = hit if hits is None else hits + hit
+        line = hits[:, 0:R]
+        for slot in range(first_slot, last_slot):
+            t = slot - first_slot
+            colmsg[own_col, pl.ds(step(z, -ORDER[slot], 8), 1), :] = sums[:, t * R:(t + 1) * R]
+            if t:
+                line = line + hits[:, t * R:(t + 1) * R]
+        rowmsg[own_row, 8:9, :] = rowmsg[own_row, 8:9, :] - 0.5 * line
+
+    def handed(slots_):
+        for slot in slots_:
+            for half, f in ((0, xh), (1, 1 - xh)):
+                arrived(("c", half, ORDER[slot]), ej.at[f, step(z, -ORDER[slot], 8)])
+
+    @pl.when(jnp.logical_not(fetches))
+    def _():
+        handed(range(5))
+
+    columns(0, 5)
+    @pl.when(fetches)
+    def _():
+        for half, f in ((0, xh), (1, 1 - xh)):
+            for k in (3, 5, 4):
+                from_z(half, f, k)
+
+    @pl.when(jnp.logical_not(fetches))
+    def _():
+        handed(range(5, 8))
+
+    columns(5, 8)
+    for p in range(8):
+        rowmsg[own_row, p:p + 1, :] = to_rows(rowacc[p * R:(p + 1) * R, :])
 
     for kz, kc in COLUMN:
         send(("col", kz, kc), colmsg.at[own_col], colmsg.at[own_col], dev(dz=kz, dc=kc))
     for ky, kx in PLANE:
         send(("row", ky, kx), rowmsg.at[own_row], rowmsg.at[own_row], dev(dy=ky, dx=kx))
+    send_hidden(3)
     for ky, kx in PLANE:
         arrived(("row", ky, kx), rowmsg.at[step(y, -ky, 4) * 4 + step(x, -kx, 4)])
     for kz, kc in COLUMN:
@@ -293,7 +310,8 @@
 
     inv_rows = 1.0 / row_total
     inv_cols = 1.0 / all_cols
-    tsum[...] = jnp.concatenate([inv_cols[t:t + 1] for t in range(8)], axis=1)
+    isum_cols[...] = inv_cols
+    tsum[...] = jnp.concatenate([isum_cols[pl.ds(step(z, -k, 8), 1), :] for k in ORDER], axis=1)
     for p in range(8):
         factor[p] = to_columns(inv_rows[p:p + 1])
     for ky in (2, 1, 3, 0):
@@ -373,13 +391,22 @@
     gemb_ref[...] = grad
     g4[0:R, :] = grad.astype(BF16)
 
-    for n, (kx, kc) in enumerate(GROUP):
-        if n:
-            send(("g", n), g4.at[0:R, :], g4.at[n * R:(n + 1) * R, :], group_dev(kx, kc))
+    def block_of(n):
+        return g4.at[n * R:(n + 1) * R, :]
+
+    def tn(a, b):
+        return lax.dot_general(a, b, (((0,), (0,)), ((), ())), preferred_element_type=F32)
+
+    send(("g", 2), block_of(0), block_of(2), group_dev(1, 0))
+    send(("g", 1), block_of(0), block_of(1), group_dev(0, 1))
     for n in range(1, 4):
         arrived(("h", n), hq.at[n * R:(n + 1) * R, :])
-        arrived(("g", n), g4.at[n * R:(n + 1) * R, :])
-    full = lax.dot_general(hq[...], g4[...], (((0,), (0,)), ((), ())), preferred_element_type=F32)
+    arrived(("g", 1), block_of(1))
+    near = tn(hq[0:2 * R, :], g4[0:2 * R, :])
+    arrived(("g", 2), block_of(2))
+    send(("g", 3), block_of(2), block_of(3), group_dev(0, 1))
+    arrived(("g", 3), block_of(3))
+    full = near + tn(hq[2 * R:, :], g4[2 * R:, :])
     gp[...] = full
     gpb[...] = full.astype(BF16)
     for ky in (2, 1, 3):
@@ -408,24 +435,34 @@
     mine = rows_of(q_me, y, z)
     for kz in (4, 3, 5, 2, 6, 1, 7):
         send(("az", kz), mine, mine, dev(dz=kz))
-    for kz in (1, 7, 2, 6, 3, 5, 4):
-        arrived(("az", kz), rows_of(q_me, y, step(z, -kz, 8)))
-
-    def to_group(ky):
-        there = rows_of(q_me, step(y, -ky, 4))
+
+    def spread(kz):
+        there = rows_of(q_me, y, step(z, -kz, 8))
+        if kz:
+            arrived(("az", kz), there)
+        for ky in (2, 1, 3):
+            send(("ay", ky, kz), there, there, dev(dy=ky))
+        send(("ax", 0, kz), there, there, group_dev(1, 0))
+
+    by_distance = (0, 1, 7, 2, 6, 3, 5, 4)
+    for kz in by_distance:
+        spread(kz)
+
+    mine = rows_of(q_me, y)
+    send(("ac", 0, 0), mine, mine, group_dev(0, 1))
+    for ky in (1, 3, 2):
+        y_from = step(y, -ky, 4)
+        for kz in by_distance:
+            arrived(("ay", ky, kz), rows_of(q_me, y_from, step(z, -kz, 8)))
+        there = rows_of(q_me, y_from)
         send(("ax", ky), there, there, group_dev(1, 0))
         send(("ac", 0, ky), there, there, group_dev(0, 1))
-
-    mine = rows_of(q_me, y)
-    for ky in (2, 1, 3):
-        send(("ay", ky), mine, mine, dev(dy=ky))
-    to_group(0)
-    for ky in (1, 3, 2):
-        arrived(("ay", ky), rows_of(q_me, step(y, -ky, 4)))
-        to_group(ky)
+    for kz in by_distance:
+        arrived(("ax", 0, kz), rows_of((1 - xl) * 2 + c, y, step(z, -kz, 8)))
     for ky in (0, 1, 3, 2):
         there = rows_of((1 - xl) * 2 + c, step(y, -ky, 4))
-        arrived(("ax", ky), there)
+        if ky:
+            arrived(("ax", ky), there)
         send(("ac", 1, ky), there, there, group_dev(0, 1))
 
     for kz, kc in COLUMN:
@@ -481,6 +518,8 @@
             vmem((16, 8, R), F32),
             vmem((16, 8, R), F32),
             vmem((1, 1024), F32),
+            vmem((8, R), F32),
+            vmem((1024, R), F32),
             vmem((8, R, R), F32),
             vmem((4, 4, H, 256), BF16),
             vmem((4, 4, H, 256), BF16),
@@ -511,9 +550,9 @@
             pltpu.SemaphoreType.DMA((COPIES,)),
         ],
         compiler_params=pltpu.CompilerParams(
-            collective_id=0, has_side_effects=True, vmem_limit_bytes=56 * 1024 * 1024
+            collective_id=0, has_side_effects=True, vmem_limit_bytes=40 * 1024 * 1024
         ),
-    )(head_hidden, proj_weight, pair_perm.reshape(64, R))
+    )(*[pltpu.with_memory_space_constraint(v, pltpu.HBM) for v in (head_hidden, proj_weight, pair_perm.reshape(64, R))])
     return loss[0, 0], grad_emb, grad_proj.astype(F32)
 
 

time: 89.3 us -> 80.9 us (0.906)
  Pallas kernels: 84 us -> 77.5 us
  other arithmetic: 2.7 us -> 1.48 us
    pallas_call x1, Pallas kernels: 84 us -> 77.5 us  [per_device(): pl.pallas_call(kernel, out_shape=(jax.ShapeDtypeStruct((8, R), F32), jax....]
    convert_element_type x1, other arithmetic: 2.7 us -> 1.48 us  [per_device(): return (loss[0, 0], grad_emb, grad_proj.astype(F32))]
where the time goes in v3:
time: 80.9 us; the launch traced here: 80.8 us
  Pallas kernels  77.5 us (96%)
  other arithmetic  1.48 us (2%)
  local copies, waits for them, and re-layouts  1.17 us (1%)
    pallas_call x1, Pallas kernels, per_device(): pl.pallas_call(kernel, out_shape=(jax.ShapeDtypeStruct((8, R), F32), jax....  77.5 us

profile of v3, /device:TPU:1, one launch (start us, length us, event | category | flops | bytes accessed | tf_op | source)
XLA Modules:
  0.0 80.8 jit_solution(14591790151651318220)
XLA Ops:
  0.6 77.5 %shard_map.58 = (f32[8,128]{1,0:T(8,128)S(1)}, f32[128,256]{1,0:T(8,128)S(1)}, bf16[2048,256]{1,0:T(8,128)(2,1)S(1)}) custom-call(bf16[128,2048]{1,0:T(8,128)(2,1)} %h_hbm.1, bf16[2048,256]{1,0:T(8,128)(2,1)} %w_hbm.1, s32[64,128]{1,0:T(8,128)} %bitcast.2), custom_call_target="tpu_custom_call" | custom-call | tf_op jit(solution)/shard_map/pallas_call | solution.py:498
  78.2 0.5 slice.3
  78.7 1.5 %convert_element_type.3 = f32[2048,256]{1,0:T(8,128)} convert(bf16[2048,256]{1,0:T(8,128)(2,1)S(1)} %get-tuple-element.8) | non-fusion elementwise | flops 524288 | bytes 3145728 | tf_op jit(solution)/shard_map/convert_element_type | solution.py:556
  80.2 0.7 copy.7

commit v4 on v3

--- a/solution.py
+++ b/solution.py
@@ -14,7 +14,7 @@
 R = 128
 H = 64
 ROWS = 16384
-COPIES = 224
+COPIES = 288
 
 
 def far(k, n):
@@ -46,7 +46,7 @@
     h_hbm, w_hbm, perm_hbm,
     loss_ref, gemb_ref, gproj_ref,
     h_ref, w_ref, perm_ref, ei, ej, ui, uj, sim, mark, rowmsg, colmsg, losses, tsum, isum_cols, rowacc, factor,
-    sa, sb, ra, rb, sa2, sb2, ra2, rb2, ia, ib, iar, ibr, ia2, ib2, iar2, ibr2, isum,
+    sa, sb, ra, rb, sa2, sb2, ra2, rb2, inner_out, inner_in,
     g4, hq, gp, gpb, ry, rz, rzb, s_in, s_out, s_back,
 ):
     dp = lax.axis_index("dp")
@@ -114,21 +114,29 @@
 
     pl.semaphore_wait(barrier, len(peers))
 
-    own = ei.at[y, x]
-    for k in (2, 1, 3):
-        send(("x", k), own, own, dev(dx=k))
-    for k in (1, 3, 2):
-        send(("y", k), own, own, dev(dy=k))
-
-    def along_z(half, f):
-        piece = ej.at[f, z]
+    def half_rows(ref, *at):
+        return [ref.at[(*at, slice(0, H))], ref.at[(*at, slice(H, R))]]
+
+    own = half_rows(ei, y, x)
+    for k, i in ((2, 0), (2, 1), (1, 0), (3, 0), (1, 1), (3, 1)):
+        send(("x", k, i), own[i], own[i], dev(dx=k))
+    for k, i in ((1, 1), (3, 1), (2, 1), (1, 0), (3, 0), (2, 0)):
+        send(("y", k, i), own[i], own[i], dev(dy=k))
+
+    def along_z(half, f, i):
+        piece = half_rows(ej, f, z)[i]
         for k in (2, 6, 1, 7):
-            copy(("z", half, k), piece, piece, dev(dz=k)).start()
-        copy(("c", half, 0), piece, piece, dev(dc=1)).start()
-
-    @pl.when(fetches)
-    def _():
-        along_z(0, xh)
+            copy(("z", half, k, i), piece, piece, dev(dz=k)).start()
+
+    def hand(half, f, k):
+        piece = ej.at[f, step(z, -k, 8)]
+        copy(("c", half, k), piece, piece, dev(dc=1)).start()
+
+    @pl.when(fetches)
+    def _():
+        along_z(0, xh, 0)
+        along_z(0, xh, 1)
+        hand(0, xh, 0)
 
     first = z < 4
     lanes = lax.broadcasted_iota(jnp.int32, (1, R), 1)
@@ -146,64 +154,71 @@
         mark[p * R:(p + 1) * R, :] = jnp.where(jnp.concatenate([a_col] * 8, axis=1) == b_row, -2.0, 0.0)
 
     def on_from_x(k):
-        piece = ei.at[y, step(x, -k, 4)]
-        arrived(("x", k), piece)
-        part = ei.at[y, step(x, -k, 4), 0:H]
+        part = half_rows(ei, y, step(x, -k, 4))[0]
+        arrived(("x", k, 0), part)
         for ky in (2, 1, 3):
             send(("xy", k, ky), part, part, dev(dy=ky))
 
     def on_from_y(k):
-        piece = ei.at[step(y, -k, 4), x]
-        arrived(("y", k), piece)
-        part = ei.at[step(y, -k, 4), x, H:R]
+        part = half_rows(ei, step(y, -k, 4), x)[1]
+        arrived(("y", k, 1), part)
         for kx in (2, 1, 3):
             send(("yx", k, kx), part, part, dev(dx=kx))
+
+    across = step(x, 2, 4)
+    on_from_x(2)
+
+    @pl.when(fetches)
+    def _():
+        ej[1 - xh, z, 0:H] = ei[y, across, 0:H]
+        along_z(1, 1 - xh, 0)
+
+    arrived(("x", 2, 1), half_rows(ei, y, across)[1])
+
+    @pl.when(fetches)
+    def _():
+        ej[1 - xh, z, H:R] = ei[y, across, H:R]
+        along_z(1, 1 - xh, 1)
+        hand(1, 1 - xh, 0)
 
     on_from_x(1)
     on_from_x(3)
     on_from_y(1)
     on_from_y(3)
-    on_from_x(2)
-
-    @pl.when(fetches)
-    def _():
-        ej[1 - xh, z] = ei[y, step(x, 2, 4)]
-        along_z(1, 1 - xh)
-
     on_from_y(2)
 
-    def hand(half, f, k):
-        piece = ej.at[f, step(z, -k, 8)]
-        copy(("c", half, k), piece, piece, dev(dc=1)).start()
-
-    def from_z(half, f, k):
-        piece = ej.at[f, step(z, -k, 8)]
-        if k == 4:
-            for s in range(2):
-                arrived(("z", half, 4, s), ej.at[f, step(z, 4, 8), s * H:(s + 1) * H])
-        else:
-            arrived(("z", half, k), piece)
+    def from_z(half, f, k, i):
+        part = half_rows(ej, f, step(z, -k, 8))[i]
+        arrived(("z", half, k, i), part)
         if k == 2:
-            copy(("z", half, 3), piece, piece, dev(dz=1)).start()
-            part = ej.at[f, step(z, -2, 8), 0:H]
-            copy(("z", half, 4, 0), part, part, dev(dz=2)).start()
+            if i == 0:
+                copy(("z", half, 4, 0), part, part, dev(dz=2)).start()
+            copy(("z", half, 3, i), part, part, dev(dz=1)).start()
         if k == 6:
-            copy(("z", half, 5), piece, piece, dev(dz=-1)).start()
-            part = ej.at[f, step(z, 2, 8), H:R]
-            copy(("z", half, 4, 1), part, part, dev(dz=-2)).start()
-        hand(half, f, k)
-
-    @pl.when(fetches)
-    def _():
-        for k in (2, 6, 1, 7):
-            from_z(0, xh, k)
-        for k in (2, 6, 1, 7):
-            from_z(1, 1 - xh, k)
-
+            if i == 1:
+                copy(("z", half, 4, 1), part, part, dev(dz=-2)).start()
+            copy(("z", half, 5, i), part, part, dev(dz=-1)).start()
+
+    @pl.when(fetches)
+    def _():
+        for half, f in ((0, xh), (1, 1 - xh)):
+            for k, i in ((2, 0), (6, 1), (2, 1), (6, 0)):
+                from_z(half, f, k, i)
+            hand(half, f, 2)
+            hand(half, f, 6)
+            for k in (1, 7):
+                from_z(half, f, k, 0)
+                from_z(half, f, k, 1)
+                hand(half, f, k)
+
+    for k in (1, 3, 2):
+        if k != 2:
+            arrived(("x", k, 1), half_rows(ei, y, step(x, -k, 4))[1])
+        arrived(("y", k, 0), half_rows(ei, step(y, -k, 4), x)[0])
     for k in (1, 3, 2):
         for j in (1, 3, 2):
-            arrived(("xy", k, j), ei.at[step(y, -j, 4), step(x, -k, 4), 0:H])
-            arrived(("yx", k, j), ei.at[step(y, -k, 4), step(x, -j, 4), H:R])
+            arrived(("xy", k, j), half_rows(ei, step(y, -j, 4), step(x, -k, 4))[0])
+            arrived(("yx", k, j), half_rows(ei, step(y, -k, 4), step(x, -j, 4))[1])
 
     def unit(dst, rows, e0, e1):
         e0 = e0.astype(F32)
@@ -278,7 +293,9 @@
     def _():
         for half, f in ((0, xh), (1, 1 - xh)):
             for k in (3, 5, 4):
-                from_z(half, f, k)
+                from_z(half, f, k, 0)
+                from_z(half, f, k, 1)
+                hand(half, f, k)
 
     @pl.when(jnp.logical_not(fetches))
     def _():
@@ -314,6 +331,10 @@
     tsum[...] = jnp.concatenate([isum_cols[pl.ds(step(z, -k, 8), 1), :] for k in ORDER], axis=1)
     for p in range(8):
         factor[p] = to_columns(inv_rows[p:p + 1])
+    def send_b(ky, kx):
+        y_to, x_to = step(y, ky, 4), step(x, kx, 4)
+        send(("rb", ky, kx), sb.at[y_to, x_to], rb.at[ky, x_to], dev(dy=ky))
+
     for ky in (2, 1, 3, 0):
         y_to = step(y, ky, 4)
         rows = pl.ds(pl.multiple_of(y_to * 256, 256), 256)
@@ -331,59 +352,55 @@
         for kx in (2, 1, 3):
             send(("ra", kx, ky), sa.at[step(x, kx, 4), y_to], ra.at[kx, y_to], dev(dx=kx))
         if ky:
-            send(("rb", ky), sb.at[y_to], rb.at[ky], dev(dy=ky))
+            send_b(ky, 2)
         for half in range(2):
             v = to_rows(acc[half * R:(half + 1) * R])
-            ia[half, pl.ds(y_to, 1), :] = v
-            ib[y_to, half:half + 1, :] = v
-        if ky:
-            send(("ib", ky), ib.at[y_to], ibr.at[ky], dev(dy=ky))
-    for kx in (2, 1, 3):
-        send(("ia", kx), ia.at[step(xl, kx, 2)], iar.at[kx], dev(dx=kx))
+            inner_out[y_to, half] = jnp.broadcast_to(v, (8, R))
+        for kx in (2, 1, 3, 0):
+            if ky or kx:
+                send(
+                    ("in", ky, kx), inner_out.at[y_to, step(xl, kx, 2)], inner_in.at[ky * 4 + kx],
+                    dev(dy=ky, dx=kx),
+                )
+    for kx in (1, 3, 0):
+        for ky in (2, 1, 3):
+            send_b(ky, kx)
     for kz, kc in COLUMN:
         send(("loss", kz, kc), losses.at[own_col], losses.at[own_col], dev(dz=kz, dc=kc))
 
-    for ky in (2, 1, 3):
-        arrived(("rb", ky), rb.at[ky])
-        arrived(("ib", ky), ibr.at[ky])
-    line = ib[y] + ibr[1] + ibr[2] + ibr[3]
-    isum[1] = line
-    for half in range(2):
-        ib2[half] = jnp.broadcast_to(line[half:half + 1], (8, R))
-    for kx in (2, 1, 3):
+    def total_a(ky):
+        y_to = step(y, ky, 4)
+        g = sa[x, y_to].astype(F32)
+        for kx in (1, 2, 3):
+            arrived(("ra", kx, ky), ra.at[kx, y_to])
+            g = g + ra[kx, y_to].astype(F32)
+        return g
+
+    def total_b(kx):
         x_to = step(x, kx, 4)
-        g = sb[y, x_to].astype(F32) + rb[1, x_to].astype(F32) + rb[2, x_to].astype(F32) + rb[3, x_to].astype(F32)
-        sb2[kx] = g.astype(BF16)
-        send(("rb2", kx), sb2.at[kx], rb2.at[kx], dev(dx=kx))
-        send(("ib2", kx), ib2.at[step(xl, kx, 2)], ibr2.at[kx], dev(dx=kx))
-    g_b = sb[y, x].astype(F32) + rb[1, x].astype(F32) + rb[2, x].astype(F32) + rb[3, x].astype(F32)
-    for kx in (2, 1, 3):
-        arrived(("ia", kx), iar.at[kx])
-        for ky in range(4):
-            arrived(("ra", kx, ky), ra.at[kx, step(y, ky, 4)])
-    line = ia[xl] + iar[1] + iar[2] + iar[3]
-    isum[0] = line
-    for yy in range(4):
-        ia2[yy] = jnp.broadcast_to(line[yy:yy + 1], (8, R))
-    for ky in (2, 1, 3):
-        y_to = step(y, ky, 4)
-        g = sa[x, y_to].astype(F32) + ra[1, y_to].astype(F32) + ra[2, y_to].astype(F32) + ra[3, y_to].astype(F32)
-        sa2[ky] = g.astype(BF16)
-        send(("ra2", ky), sa2.at[ky], ra2.at[ky], dev(dy=ky))
-        send(("ia2", ky), ia2.at[y_to], iar2.at[ky], dev(dy=ky))
-    g_a = sa[x, y].astype(F32) + ra[1, y].astype(F32) + ra[2, y].astype(F32) + ra[3, y].astype(F32)
-    inner_a = isum[0, pl.ds(y, 1), :]
-    inner_b = isum[1, pl.ds(xl, 1), :]
-    for k in (1, 3, 2):
+        g = sb[y, x_to].astype(F32)
+        for ky in (1, 2, 3):
+            arrived(("rb", ky, kx), rb.at[ky, x_to])
+            g = g + rb[ky, x_to].astype(F32)
+        return g
+
+    for k in (2, 1, 3):
+        sa2[k] = total_a(k).astype(BF16)
+        send(("ra2", k), sa2.at[k], ra2.at[k], dev(dy=k))
+        sb2[k] = total_b(k).astype(BF16)
+        send(("rb2", k), sb2.at[k], rb2.at[k], dev(dx=k))
+    g_a = total_a(0)
+    g_b = total_b(0)
+    inner = inner_out[y, xl, 0:1]
+    for ky, kx in PLANE:
+        arrived(("in", ky, kx), inner_in.at[ky * 4 + kx])
+        inner = inner + inner_in[ky * 4 + kx, 0:1]
+    for k in (2, 1, 3):
+        arrived(("ra2", k), ra2.at[k])
         arrived(("rb2", k), rb2.at[k])
-        arrived(("ib2", k), ibr2.at[k])
-        arrived(("ra2", k), ra2.at[k])
-        arrived(("ia2", k), iar2.at[k])
         g_a = g_a + ra2[k].astype(F32)
         g_b = g_b + rb2[k].astype(F32)
-        inner_a = inner_a + iar2[k, 0:1]
-        inner_b = inner_b + ibr2[k, 0:1]
-    inner = to_columns(jnp.where(lanes < H, inner_a, inner_b))
+    inner = to_columns(inner)
     inv = inverse_norm(ei[y, xl].astype(F32), ei[y, 2 + xl].astype(F32))
     own_unit = ei[y, x].astype(F32) * inv
     g = jnp.concatenate([g_a, g_b], axis=0)
@@ -409,19 +426,20 @@
     full = near + tn(hq[2 * R:, :], g4[2 * R:, :])
     gp[...] = full
     gpb[...] = full.astype(BF16)
-    for ky in (2, 1, 3):
-        part = gpb.at[pl.ds(pl.multiple_of(step(y, ky, 4) * R, R), R), :]
-        send(("gy", ky), part, ry.at[ky], dev(dy=ky))
-    part = gp[pl.ds(pl.multiple_of(y * R, R), R), :]
-    for ky in (1, 3, 2):
-        arrived(("gy", ky), ry.at[ky])
-        part = part + ry[ky].astype(F32)
-    gp[0:R, :] = part
-    rzb[...] = part.astype(BF16)
-    for kz in (4, 3, 5, 2, 6, 1, 7):
-        piece = rzb.at[pl.ds(pl.multiple_of(step(z, kz, 8) * 16, 16), 16), :]
-        send(("gz", kz), piece, rz.at[kz], dev(dz=kz))
-    piece = gp[pl.ds(pl.multiple_of(z * 16, 16), 16), :]
+    def piece_at(kz, ky):
+        return pl.ds(pl.multiple_of(step(y, ky, 4) * R + step(z, kz, 8) * 16, 16), 16)
+
+    for kz in (4, 3, 5, 2, 6, 1, 7, 0):
+        for ky in (2, 1, 3):
+            send(("gy", ky, kz), gpb.at[piece_at(kz, ky), :], ry.at[ky, kz], dev(dy=ky))
+    for kz in (4, 3, 5, 2, 6, 1, 7, 0):
+        piece = gp[piece_at(kz, 0), :]
+        for ky in (1, 3, 2):
+            arrived(("gy", ky, kz), ry.at[ky, kz])
+            piece = piece + ry[ky, kz].astype(F32)
+        if kz:
+            rzb[kz] = piece.astype(BF16)
+            send(("gz", kz), rzb.at[kz], rz.at[kz], dev(dz=kz))
     for kz in (1, 7, 2, 6, 3, 5, 4):
         arrived(("gz", kz), rz.at[kz])
         piece = piece + rz[kz].astype(F32)
@@ -481,12 +499,11 @@
     @pl.when(fetches)
     def _():
         whole = ej.at[0, 0]
-        half_piece = ej.at[0, 0, 0:H]
+        part = ej.at[0, 0, 0:H]
         for half in range(2):
-            for k in (2, 6, 1, 7, 3, 5):
-                copy(("z", half, k), whole, whole, dev(dc=1)).wait_send()
-            for s in range(2):
-                copy(("z", half, 4, s), half_piece, half_piece, dev(dc=1)).wait_send()
+            for k in range(1, 8):
+                for i in range(2):
+                    copy(("z", half, k, i), part, part, dev(dc=1)).wait_send()
             for k in range(8):
                 copy(("c", half, k), whole, whole, dev(dc=1)).wait_send()
 
@@ -529,22 +546,15 @@
             vmem((4, H, 256), BF16),
             vmem((4, H, 256), BF16),
             vmem((4, H, 256), BF16),
-            vmem((2, 8, R), F32),
-            vmem((4, 8, R), F32),
-            vmem((4, 8, R), F32),
-            vmem((4, 8, R), F32),
-            vmem((4, 8, R), F32),
-            vmem((2, 8, R), F32),
-            vmem((4, 8, R), F32),
-            vmem((4, 8, R), F32),
-            vmem((2, 8, R), F32),
+            vmem((4, 2, 8, R), F32),
+            vmem((16, 8, R), F32),
             vmem((512, 256), BF16),
             vmem((512, 512), BF16),
             vmem((512, 256), F32),
             vmem((512, 256), BF16),
-            vmem((4, R, 256), BF16),
+            vmem((4, 8, 16, 256), BF16),
             vmem((8, 16, 256), BF16),
-            vmem((R, 256), BF16),
+            vmem((8, 16, 256), BF16),
             pltpu.SemaphoreType.DMA((3,)),
             pltpu.SemaphoreType.DMA((COPIES,)),
             pltpu.SemaphoreType.DMA((COPIES,)),

time: 80.9 us -> 78.5 us (0.970)
  Pallas kernels: 77.5 us -> 75.1 us
    pallas_call x1, Pallas kernels: 77.5 us -> 75.1 us  [per_device(): pl.pallas_call(kernel, out_shape=(jax.ShapeDtypeStruct((8, R), F32), jax....]
where the time goes in v4:
time: 78.5 us; the launch traced here: 78.4 us
  Pallas kernels  75.1 us (96%)
  other arithmetic  1.48 us (2%)
  local copies, waits for them, and re-layouts  1.17 us (1%)
    pallas_call x1, Pallas kernels, per_device(): pl.pallas_call(kernel, out_shape=(jax.ShapeDtypeStruct((8, R), F32), jax....  75.1 us

profile of v4, /device:TPU:1, one launch (start us, length us, event | category | flops | bytes accessed | tf_op | source)
XLA Modules:
  0.0 78.4 jit_solution(1610531486217793763)
XLA Ops:
  0.6 75.1 %shard_map.58 = (f32[8,128]{1,0:T(8,128)S(1)}, f32[128,256]{1,0:T(8,128)S(1)}, bf16[2048,256]{1,0:T(8,128)(2,1)S(1)}) custom-call(bf16[128,2048]{1,0:T(8,128)(2,1)} %h_hbm.1, bf16[2048,256]{1,0:T(8,128)(2,1)} %w_hbm.1, s32[64,128]{1,0:T(8,128)} %bitcast.2), custom_call_target="tpu_custom_call" | custom-call | tf_op jit(solution)/shard_map/pallas_call | solution.py:515
  75.8 0.5 slice.3
  76.3 1.5 %convert_element_type.3 = f32[2048,256]{1,0:T(8,128)} convert(bf16[2048,256]{1,0:T(8,128)(2,1)S(1)} %get-tuple-element.8) | non-fusion elementwise | flops 524288 | bytes 3145728 | tf_op jit(solution)/shard_map/convert_element_type | solution.py:566
  77.7 0.7 copy.7

commit v5 on v4

--- a/solution.py
+++ b/solution.py
@@ -14,7 +14,7 @@
 R = 128
 H = 64
 ROWS = 16384
-COPIES = 288
+COPIES = 320
 
 
 def far(k, n):
@@ -23,7 +23,6 @@
 
 PLANE = sorted([(ky, kx) for ky in range(4) for kx in range(4)][1:], key=lambda k: -far(k[0], 4) - far(k[1], 4))
 COLUMN = sorted([(kz, kc) for kz in range(8) for kc in range(2)][1:], key=lambda k: -far(k[0], 8))
-GROUP = [(kx, kc) for kx in range(2) for kc in range(2)]
 
 
 def nt(a, b):
@@ -47,7 +46,7 @@
     loss_ref, gemb_ref, gproj_ref,
     h_ref, w_ref, perm_ref, ei, ej, ui, uj, sim, mark, rowmsg, colmsg, losses, tsum, isum_cols, rowacc, factor,
     sa, sb, ra, rb, sa2, sb2, ra2, rb2, inner_out, inner_in,
-    g4, hq, gp, gpb, ry, rz, rzb, s_in, s_out, s_back,
+    gout, g4, hq, gp, gpb, ry, rz, rzb, s_in, s_out, s_back,
 ):
     dp = lax.axis_index("dp")
     xh = lax.axis_index("mp")
@@ -57,7 +56,6 @@
     z = dp // 16
     x = xh * 2 + xl
     p_me = y * 2 + xl
-    q_me = xl * 2 + c
     fetches = c == xh
 
     def dev(dz=0, dy=0, dx=0, dc=0):
@@ -68,8 +66,7 @@
         k = k % n
         return v if k == 0 else lax.rem(v + k, n)
 
-    def group_dev(kx, kc):
-        return (((z * 4 + y) * 2 + step(xl, kx, 2)) * 2 + step(c, kc, 2), xh)
+    neighbour = (((z * 4 + y) * 2 + (1 - xl)) * 2 + c, xh)
 
     slots = {}
 
@@ -90,23 +87,30 @@
     def arrived(key, dst):
         copy(key, dst, dst, dev(dc=1)).wait_recv()
 
-    loads = [
-        pltpu.make_async_copy(h_hbm, h_ref, s_in.at[0]),
-        pltpu.make_async_copy(w_hbm, w_ref, s_in.at[1]),
-        pltpu.make_async_copy(perm_hbm, perm_ref, s_in.at[2]),
-    ]
+    depth = 512
+    parts = [slice(k * depth, (k + 1) * depth) for k in range(2048 // depth)]
+    loads = []
+    for n, part in enumerate(parts):
+        loads.append(pltpu.make_async_copy(h_hbm.at[:, part], h_ref.at[:, part], s_in.at[2 * n]))
+        loads.append(pltpu.make_async_copy(w_hbm.at[part, :], w_ref.at[part, :], s_in.at[2 * n + 1]))
+    loads.append(pltpu.make_async_copy(perm_hbm, perm_ref, s_in.at[2 * len(parts)]))
     for load in loads:
         load.start()
 
     barrier = pltpu.get_barrier_semaphore()
-    peers = [dev(dz=kz, dc=kc) for kz, kc in COLUMN] + [dev(dy=ky, dx=kx) for ky, kx in PLANE] + [group_dev(1, 1)]
+    peers = [dev(dz=kz, dc=kc) for kz, kc in COLUMN] + [dev(dy=ky, dx=kx) for ky, kx in PLANE]
+    peers += [dev(dx=1, dc=1), dev(dx=3, dc=1)]
     for peer in peers:
         pl.semaphore_signal(barrier, inc=1, device_id=peer, device_id_type=MESH)
-    for load in loads:
-        load.wait()
-
-    embed = jnp.dot(h_ref[...], w_ref[...], preferred_element_type=F32).astype(BF16)
-    ei[y, x] = embed
+
+    total = None
+    for n, part in enumerate(parts):
+        loads[2 * n].wait()
+        loads[2 * n + 1].wait()
+        product = jnp.dot(h_ref[:, part], w_ref[part, :], preferred_element_type=F32)
+        total = product if total is None else total + product
+    ei[y, x] = total.astype(BF16)
+    loads[-1].wait()
 
     @pl.when(fetches)
     def _():
@@ -211,15 +215,6 @@
                 from_z(half, f, k, 1)
                 hand(half, f, k)
 
-    for k in (1, 3, 2):
-        if k != 2:
-            arrived(("x", k, 1), half_rows(ei, y, step(x, -k, 4))[1])
-        arrived(("y", k, 0), half_rows(ei, step(y, -k, 4), x)[0])
-    for k in (1, 3, 2):
-        for j in (1, 3, 2):
-            arrived(("xy", k, j), half_rows(ei, step(y, -j, 4), step(x, -k, 4))[0])
-            arrived(("yx", k, j), half_rows(ei, step(y, -k, 4), step(x, -j, 4))[1])
-
     def unit(dst, rows, e0, e1):
         e0 = e0.astype(F32)
         e1 = e1.astype(F32)
@@ -227,50 +222,41 @@
         dst[0, rows, :] = (e0 * inv).astype(BF16)
         dst[1, rows, :] = (e1 * inv).astype(BF16)
 
-    for p in range(8):
-        unit(ui, slice(p * R, (p + 1) * R), ei[p // 2, p % 2], ei[p // 2, 2 + p % 2])
-
-    def send_hidden(n):
-        kx, kc = GROUP[n]
-        q = step(xl, kx, 2) * 2 + step(c, kc, 2)
-        quarter_columns = pl.ds(pl.multiple_of(q * 512, 512), 512)
-        if n == 0:
-            hq[0:R, :] = h_ref[:, quarter_columns]
-        else:
-            send(("h", n), h_ref.at[:, quarter_columns], hq.at[n * R:(n + 1) * R, :], group_dev(kx, kc))
-
-    for n in range(3):
-        send_hidden(n)
+    def unit_columns(slots_):
+        for slot in slots_:
+            zz = step(z, -ORDER[slot], 8)
+            unit(uj, slice(slot * R, (slot + 1) * R), ej[0, zz], ej[1, zz])
+
+    def handed(slots_):
+        for slot in slots_:
+            for half, f in ((0, xh), (1, 1 - xh)):
+                arrived(("c", half, ORDER[slot]), ej.at[f, step(z, -ORDER[slot], 8)])
 
     own_row = y * 4 + x
     own_col = z * 2 + c
-    rowacc[...] = jnp.zeros_like(rowacc)
     rowmsg[own_row] = jnp.zeros((16, R), F32)
 
-    def columns(first_slot, last_slot):
-        for slot in range(first_slot, last_slot):
-            zz = step(z, -ORDER[slot], 8)
-            unit(uj, slice(slot * R, (slot + 1) * R), ej[0, zz], ej[1, zz])
+    def scores(first_slot, last_slot, ky, so_far):
+        y_from = step(y, -ky, 4)
+        rows = pl.ds(pl.multiple_of(y_from * 256, 256), 256)
         cols = slice(first_slot * R, last_slot * R)
-        sums = None
-        hits = None
-        for b in range(4):
-            rows = slice(b * 256, (b + 1) * 256)
-            s = nt(ui[0, rows, :], uj[0, cols, :]) + nt(ui[1, rows, :], uj[1, cols, :])
-            hit = jnp.sum(s * mark[rows, cols], axis=0, keepdims=True)
-            e = jnp.exp2(EXP2_SCALE * s - EXP2_SCALE)
-            if first_slot == 0:
-                at = lax.broadcasted_iota(jnp.int32, (256, R), 0) - lax.broadcasted_iota(jnp.int32, (256, R), 1)
-                diagonal = at == jnp.where(fetches, p_me * R - b * 256, -ROWS)
-                e = jnp.concatenate([jnp.where(diagonal, 0.0, e[:, 0:R]), e[:, R:]], axis=1)
-            sim[rows, cols] = e
-            part = e[:, 0:R]
-            for t in range(1, last_slot - first_slot):
-                part = part + e[:, t * R:(t + 1) * R]
-            rowacc[rows, :] = rowacc[rows, :] + part
-            total = jnp.sum(e, axis=0, keepdims=True)
-            sums = total if sums is None else sums + total
-            hits = hit if hits is None else hits + hit
+        s = nt(ui[0, rows, :], uj[0, cols, :]) + nt(ui[1, rows, :], uj[1, cols, :])
+        hit = jnp.sum(s * mark[rows, cols], axis=0, keepdims=True)
+        e = jnp.exp2(EXP2_SCALE * s - EXP2_SCALE)
+        if first_slot == 0 and ky == 0:
+            at = lax.broadcasted_iota(jnp.int32, (256, R), 0) - lax.broadcasted_iota(jnp.int32, (256, R), 1)
+            diagonal = at == jnp.where(fetches, xl * R, -ROWS)
+            e = jnp.concatenate([jnp.where(diagonal, 0.0, e[:, 0:R]), e[:, R:]], axis=1)
+        sim[rows, cols] = e
+        part = e[:, 0:R]
+        for t in range(1, last_slot - first_slot):
+            part = part + e[:, t * R:(t + 1) * R]
+        rowacc[rows, :] = part if first_slot == 0 else rowacc[rows, :] + part
+        total = jnp.sum(e, axis=0, keepdims=True)
+        return (total, hit) if so_far is None else (so_far[0] + total, so_far[1] + hit)
+
+    def hand_in(first_slot, last_slot, so_far):
+        sums, hits = so_far
         line = hits[:, 0:R]
         for slot in range(first_slot, last_slot):
             t = slot - first_slot
@@ -279,16 +265,44 @@
                 line = line + hits[:, t * R:(t + 1) * R]
         rowmsg[own_row, 8:9, :] = rowmsg[own_row, 8:9, :] - 0.5 * line
 
-    def handed(slots_):
-        for slot in slots_:
-            for half, f in ((0, xh), (1, 1 - xh)):
-                arrived(("c", half, ORDER[slot]), ej.at[f, step(z, -ORDER[slot], 8)])
-
     @pl.when(jnp.logical_not(fetches))
     def _():
         handed(range(5))
 
-    columns(0, 5)
+    unit_columns(range(5))
+    so_far = None
+    for ky in (0, 1, 3, 2):
+        y_from = step(y, -ky, 4)
+        if ky == 0:
+            for k in (1, 3):
+                arrived(("x", k, 1), half_rows(ei, y, step(x, -k, 4))[1])
+        else:
+            arrived(("y", ky, 0), half_rows(ei, y_from, x)[0])
+            for k in (1, 3, 2):
+                arrived(("xy", k, ky), half_rows(ei, y_from, step(x, -k, 4))[0])
+                arrived(("yx", ky, k), half_rows(ei, y_from, step(x, -k, 4))[1])
+        for half in range(2):
+            rows = pl.ds(pl.multiple_of(y_from * 256 + half * R, R), R)
+            unit(ui, rows, ei[y_from, half], ei[y_from, 2 + half])
+        so_far = scores(0, 5, ky, so_far)
+    hand_in(0, 5, so_far)
+
+    def hidden_rows(kc, x_):
+        return pl.ds(pl.multiple_of((kc * 2 + x_) * R, R), R)
+
+    def half_of(core):
+        return pl.ds(pl.multiple_of(core * 1024, 1024), 1024)
+
+    def send_hidden(kc):
+        for n, dx in ((0, 1), (1, 3)):
+            cols = pl.ds(pl.multiple_of(step(c, kc, 2) * 1024 + n * 512, 512), 512)
+            there = hq.at[hidden_rows(kc, xl), n * 512:(n + 1) * 512]
+            send(("hx", n, kc), h_ref.at[:, cols], there, dev(dx=dx, dc=kc))
+
+    hq[hidden_rows(0, xl), :] = h_ref[:, half_of(c)]
+    send(("h",), h_ref.at[:, half_of(1 - c)], hq.at[hidden_rows(1, xl), :], dev(dc=1))
+    send_hidden(0)
+
     @pl.when(fetches)
     def _():
         for half, f in ((0, xh), (1, 1 - xh)):
@@ -301,7 +315,11 @@
     def _():
         handed(range(5, 8))
 
-    columns(5, 8)
+    unit_columns(range(5, 8))
+    so_far = None
+    for ky in (0, 1, 3, 2):
+        so_far = scores(5, 8, ky, so_far)
+    hand_in(5, 8, so_far)
     for p in range(8):
         rowmsg[own_row, p:p + 1, :] = to_rows(rowacc[p * R:(p + 1) * R, :])
 
@@ -309,7 +327,7 @@
         send(("col", kz, kc), colmsg.at[own_col], colmsg.at[own_col], dev(dz=kz, dc=kc))
     for ky, kx in PLANE:
         send(("row", ky, kx), rowmsg.at[own_row], rowmsg.at[own_row], dev(dy=ky, dx=kx))
-    send_hidden(3)
+    send_hidden(1)
     for ky, kx in PLANE:
         arrived(("row", ky, kx), rowmsg.at[step(y, -ky, 4) * 4 + step(x, -kx, 4)])
     for kz, kc in COLUMN:
@@ -343,9 +361,9 @@
         acc = None
         for f in range(2):
             g = jnp.dot(weights, uj[f], preferred_element_type=F32)
-            for half in range(2):
-                sa[2 * f + half, y_to] = g[half * R:half * R + H].astype(BF16)
-                sb[y_to, 2 * f + half] = g[half * R + H:(half + 1) * R].astype(BF16)
+            for q in range(2):
+                sa[2 * f + q, y_to] = g[0:R, q * R:(q + 1) * R].astype(BF16)
+                sb[y_to, 2 * f + q] = g[R:2 * R, q * R:(q + 1) * R].astype(BF16)
             t = g * ui[f, rows, :].astype(F32)
             t = t[:, 0:R] + t[:, R:]
             acc = t if acc is None else acc + t
@@ -355,11 +373,11 @@
             send_b(ky, 2)
         for half in range(2):
             v = to_rows(acc[half * R:(half + 1) * R])
-            inner_out[y_to, half] = jnp.broadcast_to(v, (8, R))
+            inner_out[y_to, half:half + 1, :] = v
         for kx in (2, 1, 3, 0):
             if ky or kx:
                 send(
-                    ("in", ky, kx), inner_out.at[y_to, step(xl, kx, 2)], inner_in.at[ky * 4 + kx],
+                    ("in", ky, kx), inner_out.at[y_to], inner_in.at[ky * 4 + kx],
                     dev(dy=ky, dx=kx),
                 )
     for kx in (1, 3, 0):
@@ -391,43 +409,40 @@
         send(("rb2", k), sb2.at[k], rb2.at[k], dev(dx=k))
     g_a = total_a(0)
     g_b = total_b(0)
-    inner = inner_out[y, xl, 0:1]
+    inner = inner_out[y]
     for ky, kx in PLANE:
         arrived(("in", ky, kx), inner_in.at[ky * 4 + kx])
-        inner = inner + inner_in[ky * 4 + kx, 0:1]
+        inner = inner + inner_in[ky * 4 + kx]
     for k in (2, 1, 3):
         arrived(("ra2", k), ra2.at[k])
         arrived(("rb2", k), rb2.at[k])
         g_a = g_a + ra2[k].astype(F32)
         g_b = g_b + rb2[k].astype(F32)
-    inner = to_columns(inner)
-    inv = inverse_norm(ei[y, xl].astype(F32), ei[y, 2 + xl].astype(F32))
-    own_unit = ei[y, x].astype(F32) * inv
-    g = jnp.concatenate([g_a, g_b], axis=0)
-    grad = (SHARPNESS * inv) * (g - own_unit * jnp.concatenate([inner, inner], axis=1))
-    gemb_ref[...] = grad
-    g4[0:R, :] = grad.astype(BF16)
-
-    def block_of(n):
-        return g4.at[n * R:(n + 1) * R, :]
+    quarter = pl.ds(pl.multiple_of(xl * R, R), R)
+    for half, g in ((0, g_a), (1, g_b)):
+        inv = inverse_norm(ei[y, half].astype(F32), ei[y, 2 + half].astype(F32))
+        some_unit = ei[y, 2 * xh + half, :, quarter].astype(F32) * inv
+        grad = (SHARPNESS * inv) * (g - some_unit * to_columns(inner[half:half + 1]))
+        g4[half * R:(half + 1) * R, :] = grad.astype(BF16)
+        gout[half] = grad
 
     def tn(a, b):
         return lax.dot_general(a, b, (((0,), (0,)), ((), ())), preferred_element_type=F32)
 
-    send(("g", 2), block_of(0), block_of(2), group_dev(1, 0))
-    send(("g", 1), block_of(0), block_of(1), group_dev(0, 1))
-    for n in range(1, 4):
-        arrived(("h", n), hq.at[n * R:(n + 1) * R, :])
-    arrived(("g", 1), block_of(1))
+    send(("g",), g4.at[0:2 * R, :], g4.at[2 * R:4 * R, :], dev(dc=1))
+    send(("ge",), gout.at[1 - xl], gemb_ref.at[:, quarter], neighbour)
+    gemb_ref[:, quarter] = gout[xl]
+    arrived(("h",), hq.at[hidden_rows(1, xl), :])
+    for kc in range(2):
+        for n in range(2):
+            arrived(("hx", n, kc), hq.at[hidden_rows(kc, 1 - xl), n * 512:(n + 1) * 512])
     near = tn(hq[0:2 * R, :], g4[0:2 * R, :])
-    arrived(("g", 2), block_of(2))
-    send(("g", 3), block_of(2), block_of(3), group_dev(0, 1))
-    arrived(("g", 3), block_of(3))
+    arrived(("g",), g4.at[2 * R:4 * R, :])
     full = near + tn(hq[2 * R:, :], g4[2 * R:, :])
     gp[...] = full
     gpb[...] = full.astype(BF16)
     def piece_at(kz, ky):
-        return pl.ds(pl.multiple_of(step(y, ky, 4) * R + step(z, kz, 8) * 16, 16), 16)
+        return pl.ds(pl.multiple_of(step(y, ky, 4) * 256 + step(z, kz, 8) * 32, 32), 32)
 
     for kz in (4, 3, 5, 2, 6, 1, 7, 0):
         for ky in (2, 1, 3):
@@ -444,44 +459,38 @@
         arrived(("gz", kz), rz.at[kz])
         piece = piece + rz[kz].astype(F32)
 
-    def rows_of(q_, y_, z_=None):
-        if z_ is None:
-            return gproj_ref.at[pl.ds(pl.multiple_of(q_ * 512 + y_ * R, R), R), :]
-        return gproj_ref.at[pl.ds(pl.multiple_of(q_ * 512 + y_ * R + z_ * 16, 16), 16), :]
-
-    gproj_ref[pl.ds(pl.multiple_of(q_me * 512 + y * R + z * 16, 16), 16), :] = piece.astype(BF16)
-    mine = rows_of(q_me, y, z)
+    def place(x_, c_, y_, z_=None):
+        rows = slice(None) if z_ is None else pl.ds(pl.multiple_of(z_ * 32, 32), 32)
+        return gproj_ref.at[c_, y_, rows, pl.ds(pl.multiple_of(x_ * R, R), R)]
+
+    gproj_ref[c, y, pl.ds(pl.multiple_of(z * 32, 32), 32), quarter] = piece.astype(BF16)
+    mine = place(xl, c, y, z)
     for kz in (4, 3, 5, 2, 6, 1, 7):
         send(("az", kz), mine, mine, dev(dz=kz))
-
-    def spread(kz):
-        there = rows_of(q_me, y, step(z, -kz, 8))
+    for kz in ORDER:
+        there = place(xl, c, y, step(z, -kz, 8))
         if kz:
             arrived(("az", kz), there)
         for ky in (2, 1, 3):
             send(("ay", ky, kz), there, there, dev(dy=ky))
-        send(("ax", 0, kz), there, there, group_dev(1, 0))
-
-    by_distance = (0, 1, 7, 2, 6, 3, 5, 4)
-    for kz in by_distance:
-        spread(kz)
-
-    mine = rows_of(q_me, y)
-    send(("ac", 0, 0), mine, mine, group_dev(0, 1))
+        send(("ax", 0, kz), there, there, neighbour)
+
+    mine = place(xl, c, y)
+    send(("ac", 0, 0), mine, mine, dev(dc=1))
     for ky in (1, 3, 2):
         y_from = step(y, -ky, 4)
-        for kz in by_distance:
-            arrived(("ay", ky, kz), rows_of(q_me, y_from, step(z, -kz, 8)))
-        there = rows_of(q_me, y_from)
-        send(("ax", ky), there, there, group_dev(1, 0))
-        send(("ac", 0, ky), there, there, group_dev(0, 1))
-    for kz in by_distance:
-        arrived(("ax", 0, kz), rows_of((1 - xl) * 2 + c, y, step(z, -kz, 8)))
+        for kz in ORDER:
+            arrived(("ay", ky, kz), place(xl, c, y_from, step(z, -kz, 8)))
+        there = place(xl, c, y_from)
+        send(("ax", ky), there, there, neighbour)
+        send(("ac", 0, ky), there, there, dev(dc=1))
+    for kz in ORDER:
+        arrived(("ax", 0, kz), place(1 - xl, c, y, step(z, -kz, 8)))
     for ky in (0, 1, 3, 2):
-        there = rows_of((1 - xl) * 2 + c, step(y, -ky, 4))
+        there = place(1 - xl, c, step(y, -ky, 4))
         if ky:
             arrived(("ax", ky), there)
-        send(("ac", 1, ky), there, there, group_dev(0, 1))
+        send(("ac", 1, ky), there, there, dev(dc=1))
 
     for kz, kc in COLUMN:
         arrived(("loss", kz, kc), losses.at[step(z, -kz, 8) * 2 + step(c, kc, 2)])
@@ -491,8 +500,10 @@
     loss_ref[...] = jnp.broadcast_to(jnp.sum(cost, axis=1, keepdims=True) * (1.0 / ROWS), (8, R))
 
     for ky in (0, 1, 3, 2):
-        arrived(("ac", 0, ky), rows_of(xl * 2 + (1 - c), step(y, -ky, 4)))
-        arrived(("ac", 1, ky), rows_of((1 - xl) * 2 + (1 - c), step(y, -ky, 4)))
+        y_from = step(y, -ky, 4)
+        arrived(("ac", 0, ky), place(xl, 1 - c, y_from))
+        arrived(("ac", 1, ky), place(1 - xl, 1 - c, y_from))
+    arrived(("ge",), gemb_ref.at[:, pl.ds(pl.multiple_of((1 - xl) * R, R), R)])
     for one in sent:
         one.wait_send()
 
@@ -506,6 +517,19 @@
                     copy(("z", half, k, i), part, part, dev(dc=1)).wait_send()
             for k in range(8):
                 copy(("c", half, k), whole, whole, dev(dc=1)).wait_send()
+
+
+def finish(loss_in, gemb_in, gproj_in, loss_out, gemb_out, gproj_out, wide, sems):
+    copies = [pltpu.make_async_copy(gemb_in, gemb_out, sems.at[8])]
+    copies[0].start()
+    for n in range(8):
+        rows = slice(n * 256, (n + 1) * 256)
+        wide[rows, :] = gproj_in[rows, :].astype(F32)
+        copies.append(pltpu.make_async_copy(wide.at[rows, :], gproj_out.at[rows, :], sems.at[n]))
+        copies[-1].start()
+    loss_out[...] = loss_in[0:1, 0:1]
+    for one in copies:
+        one.wait()
 
 
 def per_device(head_hidden, proj_weight, pair_perm):
@@ -517,7 +541,7 @@
         out_shape=(
             jax.ShapeDtypeStruct((8, R), F32),
             jax.ShapeDtypeStruct((R, 256), F32),
-            jax.ShapeDtypeStruct((2048, 256), BF16),
+            jax.ShapeDtypeStruct((2, 4, 256, 256), BF16),
         ),
         in_specs=[hbm] * 3,
         out_specs=[space] * 3,
@@ -538,24 +562,25 @@
             vmem((8, R), F32),
             vmem((1024, R), F32),
             vmem((8, R, R), F32),
-            vmem((4, 4, H, 256), BF16),
-            vmem((4, 4, H, 256), BF16),
-            vmem((4, 4, H, 256), BF16),
-            vmem((4, 4, H, 256), BF16),
-            vmem((4, H, 256), BF16),
-            vmem((4, H, 256), BF16),
-            vmem((4, H, 256), BF16),
-            vmem((4, H, 256), BF16),
-            vmem((4, 2, 8, R), F32),
+            vmem((4, 4, R, R), BF16),
+            vmem((4, 4, R, R), BF16),
+            vmem((4, 4, R, R), BF16),
+            vmem((4, 4, R, R), BF16),
+            vmem((4, R, R), BF16),
+            vmem((4, R, R), BF16),
+            vmem((4, R, R), BF16),
+            vmem((4, R, R), BF16),
+            vmem((4, 8, R), F32),
             vmem((16, 8, R), F32),
-            vmem((512, 256), BF16),
-            vmem((512, 512), BF16),
-            vmem((512, 256), F32),
-            vmem((512, 256), BF16),
-            vmem((4, 8, 16, 256), BF16),
-            vmem((8, 16, 256), BF16),
-            vmem((8, 16, 256), BF16),
-            pltpu.SemaphoreType.DMA((3,)),
+            vmem((2, R, R), F32),
+            vmem((512, R), BF16),
+            vmem((512, 1024), BF16),
+            vmem((1024, R), F32),
+            vmem((1024, R), BF16),
+            vmem((4, 8, 32, R), BF16),
+            vmem((8, 32, R), BF16),
+            vmem((8, 32, R), BF16),
+            pltpu.SemaphoreType.DMA((9,)),
             pltpu.SemaphoreType.DMA((COPIES,)),
             pltpu.SemaphoreType.DMA((COPIES,)),
         ],
@@ -563,7 +588,20 @@
             collective_id=0, has_side_effects=True, vmem_limit_bytes=40 * 1024 * 1024
         ),
     )(*[pltpu.with_memory_space_constraint(v, pltpu.HBM) for v in (head_hidden, proj_weight, pair_perm.reshape(64, R))])
-    return loss[0, 0], grad_emb, grad_proj.astype(F32)
+    hbm = pl.BlockSpec(memory_space=pl.ANY)
+    loss, grad_emb, grad_proj = pl.pallas_call(
+        finish,
+        out_shape=(
+            jax.ShapeDtypeStruct((1, 1), F32),
+            jax.ShapeDtypeStruct((R, 256), F32),
+            jax.ShapeDtypeStruct((2048, 256), F32),
+        ),
+        in_specs=[space] * 3,
+        out_specs=[space, hbm, hbm],
+        scratch_shapes=[vmem((2048, 256), F32), pltpu.SemaphoreType.DMA((9,))],
+        compiler_params=pltpu.CompilerParams(vmem_limit_bytes=16 * 1024 * 1024),
+    )(loss, grad_emb, grad_proj.reshape(2048, 256))
+    return loss[0, 0], grad_emb, grad_proj
 
 
 def solution(mesh):

time: 78.5 us -> 74.6 us (0.950)
  other arithmetic: 1.48 us -> 0 us
  Pallas kernels: 75.1 us -> 73.8 us
  local copies, waits for them, and re-layouts: 1.17 us -> 0 us
    pallas_call x1, Pallas kernels: 75.1 us -> 71.9 us  [per_device(): pl.pallas_call(kernel, out_shape=(jax.ShapeDtypeStruct((8, R), F32), jax....]
    pallas_call x0 -> x1, Pallas kernels: none -> 1.94 us  [per_device(): pl.pallas_call(finish, out_shape=(jax.ShapeDtypeStruct((1, 1), F32), jax....]
    convert_element_type x1 -> x0, other arithmetic: 1.48 us -> none  [per_device(): return (loss[0, 0], grad_emb, grad_proj.astype(F32))]
where the time goes in v5:
time: 74.6 us; the launch traced here: 74.5 us
  Pallas kernels  73.8 us (99%)
    pallas_call x1, Pallas kernels, per_device(): pl.pallas_call(kernel, out_shape=(jax.ShapeDtypeStruct((8, R), F32), jax....  71.9 us
    pallas_call x1, Pallas kernels, per_device(): pl.pallas_call(finish, out_shape=(jax.ShapeDtypeStruct((1, 1), F32), jax....  1.94 us

profile of v5, /device:TPU:1, one launch (start us, length us, event | category | flops | bytes accessed | tf_op | source)
XLA Modules:
  0.0 74.5 jit_solution(6104648574315118084)
XLA Ops:
  0.6 71.9 %shard_map.58 = (f32[8,128]{1,0:T(8,128)S(1)}, f32[128,256]{1,0:T(8,128)S(1)}, bf16[2,4,256,256]{3,2,1,0:T(8,128)(2,1)S(1)}) custom-call(bf16[128,2048]{1,0:T(8,128)(2,1)} %h_hbm.1, bf16[2048,256]{1,0:T(8,128)(2,1)} %w_hbm.1, s32[64,128]{1,0:T(8,128)} %bitcast.4), custom_call_target="tpu_custom_call" | custom-call | tf_op jit(solution)/shard_map/pallas_call | solution.py:539
  72.5 1.9 %shard_map.59 = (f32[1,1]{1,0:T(1,128)}, f32[128,256]{1,0:T(8,128)}, f32[2048,256]{1,0:T(8,128)}) custom-call(f32[8,128]{1,0:T(8,128)S(1)} %get-tuple-element.9.loss_in, f32[128,256]{1,0:T(8,128)S(1)} %get-tuple-element.10.gemb_in, bf16[2048,256]{1,0:T(8,128)(2,1)S(1)} %bitcast.3), custom_call_target="tpu_custom_call" | custom-call | tf_op jit(solution)/shard_map/pallas_call | solution.py:592

commit v6 on v5

--- a/solution.py
+++ b/solution.py
@@ -66,7 +66,10 @@
         k = k % n
         return v if k == 0 else lax.rem(v + k, n)
 
-    neighbour = (((z * 4 + y) * 2 + (1 - xl)) * 2 + c, xh)
+    def pair_dev(kz):
+        return (((step(z, kz, 8) * 4 + y) * 2 + (1 - xl)) * 2 + c, xh)
+
+    neighbour = pair_dev(0)
 
     slots = {}
 
@@ -83,6 +86,11 @@
         one = copy(key, src, dst, to)
         one.start()
         sent.append(one)
+
+    def flush(start, stop):
+        for one in sent[start:stop]:
+            one.wait_send()
+        del sent[start:stop]
 
     def arrived(key, dst):
         copy(key, dst, dst, dev(dc=1)).wait_recv()
@@ -98,8 +106,7 @@
         load.start()
 
     barrier = pltpu.get_barrier_semaphore()
-    peers = [dev(dz=kz, dc=kc) for kz, kc in COLUMN] + [dev(dy=ky, dx=kx) for ky, kx in PLANE]
-    peers += [dev(dx=1, dc=1), dev(dx=3, dc=1)]
+    peers = [dev(dx=k) for k in (2, 1, 3)] + [dev(dy=k) for k in (2, 1, 3)] + [dev(dz=k) for k in (2, 6, 1, 7)] + [dev(dc=1)]
     for peer in peers:
         pl.semaphore_signal(barrier, inc=1, device_id=peer, device_id_type=MESH)
 
@@ -352,6 +359,8 @@
     def send_b(ky, kx):
         y_to, x_to = step(y, ky, 4), step(x, kx, 4)
         send(("rb", ky, kx), sb.at[y_to, x_to], rb.at[ky, x_to], dev(dy=ky))
+
+    older = len(sent)
 
     for ky in (2, 1, 3, 0):
         y_to = step(y, ky, 4)
@@ -386,6 +395,18 @@
     for kz, kc in COLUMN:
         send(("loss", kz, kc), losses.at[own_col], losses.at[own_col], dev(dz=kz, dc=kc))
 
+    flush(0, older)
+
+    @pl.when(fetches)
+    def _():
+        whole = ej.at[0, 0]
+        part = ej.at[0, 0, 0:H]
+        for half in range(2):
+            for k in range(1, 8):
+                for i in range(2):
+                    copy(("z", half, k, i), part, part, dev(dc=1)).wait_send()
+            for k in range(8):
+                copy(("c", half, k), whole, whole, dev(dc=1)).wait_send()
     def total_a(ky):
         y_to = step(y, ky, 4)
         g = sa[x, y_to].astype(F32)
@@ -447,6 +468,7 @@
     for kz in (4, 3, 5, 2, 6, 1, 7, 0):
         for ky in (2, 1, 3):
             send(("gy", ky, kz), gpb.at[piece_at(kz, ky), :], ry.at[ky, kz], dev(dy=ky))
+    older = len(sent)
     for kz in (4, 3, 5, 2, 6, 1, 7, 0):
         piece = gp[piece_at(kz, 0), :]
         for ky in (1, 3, 2):
@@ -455,43 +477,6 @@
         if kz:
             rzb[kz] = piece.astype(BF16)
             send(("gz", kz), rzb.at[kz], rz.at[kz], dev(dz=kz))
-    for kz in (1, 7, 2, 6, 3, 5, 4):
-        arrived(("gz", kz), rz.at[kz])
-        piece = piece + rz[kz].astype(F32)
-
-    def place(x_, c_, y_, z_=None):
-        rows = slice(None) if z_ is None else pl.ds(pl.multiple_of(z_ * 32, 32), 32)
-        return gproj_ref.at[c_, y_, rows, pl.ds(pl.multiple_of(x_ * R, R), R)]
-
-    gproj_ref[c, y, pl.ds(pl.multiple_of(z * 32, 32), 32), quarter] = piece.astype(BF16)
-    mine = place(xl, c, y, z)
-    for kz in (4, 3, 5, 2, 6, 1, 7):
-        send(("az", kz), mine, mine, dev(dz=kz))
-    for kz in ORDER:
-        there = place(xl, c, y, step(z, -kz, 8))
-        if kz:
-            arrived(("az", kz), there)
-        for ky in (2, 1, 3):
-            send(("ay", ky, kz), there, there, dev(dy=ky))
-        send(("ax", 0, kz), there, there, neighbour)
-
-    mine = place(xl, c, y)
-    send(("ac", 0, 0), mine, mine, dev(dc=1))
-    for ky in (1, 3, 2):
-        y_from = step(y, -ky, 4)
-        for kz in ORDER:
-            arrived(("ay", ky, kz), place(xl, c, y_from, step(z, -kz, 8)))
-        there = place(xl, c, y_from)
-        send(("ax", ky), there, there, neighbour)
-        send(("ac", 0, ky), there, there, dev(dc=1))
-    for kz in ORDER:
-        arrived(("ax", 0, kz), place(1 - xl, c, y, step(z, -kz, 8)))
-    for ky in (0, 1, 3, 2):
-        there = place(1 - xl, c, step(y, -ky, 4))
-        if ky:
-            arrived(("ax", ky), there)
-        send(("ac", 1, ky), there, there, dev(dc=1))
-
     for kz, kc in COLUMN:
         arrived(("loss", kz, kc), losses.at[step(z, -kz, 8) * 2 + step(c, kc, 2)])
     cost = losses[0]
@@ -499,35 +484,74 @@
         cost = cost + losses[n]
     loss_ref[...] = jnp.broadcast_to(jnp.sum(cost, axis=1, keepdims=True) * (1.0 / ROWS), (8, R))
 
+    flush(0, older)
+    for kz in (1, 7, 2, 6, 3, 5, 4):
+        arrived(("gz", kz), rz.at[kz])
+        piece = piece + rz[kz].astype(F32)
+
+    def place(x_, c_, y_, z_=None):
+        rows = slice(None) if z_ is None else pl.ds(pl.multiple_of(z_ * 32, 32), 32)
+        return gproj_ref.at[c_, y_, rows, pl.ds(pl.multiple_of(x_ * R, R), R)]
+
+    gproj_ref[c, y, pl.ds(pl.multiple_of(z * 32, 32), 32), quarter] = piece.astype(BF16)
+    def both(c_, y_, z_=None):
+        rows = slice(None) if z_ is None else pl.ds(pl.multiple_of(z_ * 32, 32), 32)
+        return gproj_ref.at[c_, y_, rows, :]
+
+    near_z, far_z = (0, 1, 7, 2, 6), (3, 5, 4)
+    mine = place(xl, c, y, z)
+    for kz in (4, 3, 5):
+        send(("az", 1, kz), mine, mine, pair_dev(kz))
+        send(("az", 0, kz), mine, mine, dev(dz=kz))
+    for kz in (2, 6, 1, 7):
+        send(("az", 0, kz), mine, mine, dev(dz=kz))
+    for kz in near_z:
+        there = place(xl, c, y, step(z, -kz, 8))
+        if kz:
+            arrived(("az", 0, kz), there)
+        for ky in (2, 1, 3):
+            send(("ay", ky, kz), there, there, dev(dy=ky))
+        send(("ax", 0, kz), there, there, neighbour)
+    for kz in far_z:
+        z_from = step(z, -kz, 8)
+        arrived(("az", 0, kz), place(xl, c, y, z_from))
+        arrived(("az", 1, kz), place(1 - xl, c, y, z_from))
+        there = both(c, y, z_from)
+        for ky in (2, 1, 3):
+            send(("ay", ky, kz), there, there, dev(dy=ky))
+    for ky in (1, 3, 2):
+        for kz in near_z:
+            there = place(xl, c, step(y, -ky, 4), step(z, -kz, 8))
+            arrived(("ay", ky, kz), there)
+            send(("ax", ky, kz), there, there, neighbour)
     for ky in (0, 1, 3, 2):
         y_from = step(y, -ky, 4)
-        arrived(("ac", 0, ky), place(xl, 1 - c, y_from))
-        arrived(("ac", 1, ky), place(1 - xl, 1 - c, y_from))
+        if ky:
+            for kz in far_z:
+                arrived(("ay", ky, kz), both(c, y_from, step(z, -kz, 8)))
+        for kz in near_z:
+            arrived(("ax", ky, kz), place(1 - xl, c, y_from, step(z, -kz, 8)))
+        send(("ac", ky), both(c, y_from), both(c, y_from), dev(dc=1))
+    for ky in (0, 1, 3, 2):
+        there = both(1 - c, step(y, -ky, 4))
+        arrived(("ac", ky), there)
     arrived(("ge",), gemb_ref.at[:, pl.ds(pl.multiple_of((1 - xl) * R, R), R)])
-    for one in sent:
-        one.wait_send()
-
-    @pl.when(fetches)
-    def _():
-        whole = ej.at[0, 0]
-        part = ej.at[0, 0, 0:H]
-        for half in range(2):
-            for k in range(1, 8):
-                for i in range(2):
-                    copy(("z", half, k, i), part, part, dev(dc=1)).wait_send()
-            for k in range(8):
-                copy(("c", half, k), whole, whole, dev(dc=1)).wait_send()
-
-
-def finish(loss_in, gemb_in, gproj_in, loss_out, gemb_out, gproj_out, wide, sems):
-    copies = [pltpu.make_async_copy(gemb_in, gemb_out, sems.at[8])]
-    copies[0].start()
+    flush(0, len(sent))
+
+
+def finish(loss_in, gemb_in, gproj_in, loss_out, gemb_out, gproj_out, wide, one_value, sems):
+    one_value[...] = loss_in[0:1, 0:1]
+    copies = [
+        pltpu.make_async_copy(gemb_in, gemb_out, sems.at[8]),
+        pltpu.make_async_copy(one_value, loss_out, sems.at[9]),
+    ]
+    for one in copies:
+        one.start()
     for n in range(8):
         rows = slice(n * 256, (n + 1) * 256)
         wide[rows, :] = gproj_in[rows, :].astype(F32)
         copies.append(pltpu.make_async_copy(wide.at[rows, :], gproj_out.at[rows, :], sems.at[n]))
         copies[-1].start()
-    loss_out[...] = loss_in[0:1, 0:1]
     for one in copies:
         one.wait()
 
@@ -597,8 +621,8 @@
             jax.ShapeDtypeStruct((2048, 256), F32),
         ),
         in_specs=[space] * 3,
-        out_specs=[space, hbm, hbm],
-        scratch_shapes=[vmem((2048, 256), F32), pltpu.SemaphoreType.DMA((9,))],
+        out_specs=[hbm, hbm, hbm],
+        scratch_shapes=[vmem((2048, 256), F32), vmem((1, 1), F32), pltpu.SemaphoreType.DMA((10,))],
         compiler_params=pltpu.CompilerParams(vmem_limit_bytes=16 * 1024 * 1024),
     )(loss, grad_emb, grad_proj.reshape(2048, 256))
     return loss[0, 0], grad_emb, grad_proj

time: 74.6 us -> 72 us (0.965)
  Pallas kernels: 73.8 us -> 71.2 us
    pallas_call x1, Pallas kernels: 71.9 us -> 69.8 us  [per_device(): pl.pallas_call(kernel, out_shape=(jax.ShapeDtypeStruct((8, R), F32), jax....]
where the time goes in v6:
time: 72 us; the launch traced here: 71.8 us
  Pallas kernels  71.2 us (99%)
    pallas_call x1, Pallas kernels, per_device(): pl.pallas_call(kernel, out_shape=(jax.ShapeDtypeStruct((8, R), F32), jax....  69.8 us
    pallas_call x1, Pallas kernels, per_device(): pl.pallas_call(finish, out_shape=(jax.ShapeDtypeStruct((1, 1), F32), jax....  1.44 us

profile of v6, /device:TPU:1, one launch (start us, length us, event | category | flops | bytes accessed | tf_op | source)
XLA Modules:
  0.0 71.8 jit_solution(359720166806313013)
XLA Ops:
  0.6 69.8 %shard_map.58 = (f32[8,128]{1,0:T(8,128)S(1)}, f32[128,256]{1,0:T(8,128)S(1)}, bf16[2,4,256,256]{3,2,1,0:T(8,128)(2,1)S(1)}) custom-call(bf16[128,2048]{1,0:T(8,128)(2,1)} %h_hbm.1, bf16[2048,256]{1,0:T(8,128)(2,1)} %w_hbm.1, s32[64,128]{1,0:T(8,128)} %bitcast.4), custom_call_target="tpu_custom_call" | custom-call | tf_op jit(solution)/shard_map/pallas_call | solution.py:563
  70.4 1.4 %shard_map.59 = (f32[1,1]{1,0:T(1,128)}, f32[128,256]{1,0:T(8,128)}, f32[2048,256]{1,0:T(8,128)}) custom-call(f32[8,128]{1,0:T(8,128)S(1)} %get-tuple-element.9.loss_in, f32[128,256]{1,0:T(8,128)S(1)} %get-tuple-element.10.gemb_in, bf16[2048,256]{1,0:T(8,128)(2,1)S(1)} %bitcast.3), custom_call_target="tpu_custom_call" | custom-call | tf_op jit(solution)/shard_map/pallas_call | solution.py:616

commit v7 on v6

--- a/solution.py
+++ b/solution.py
@@ -44,7 +44,7 @@
 def kernel(
     h_hbm, w_hbm, perm_hbm,
     loss_ref, gemb_ref, gproj_ref,
-    h_ref, w_ref, perm_ref, ei, ej, ui, uj, sim, mark, rowmsg, colmsg, losses, tsum, isum_cols, rowacc, factor,
+    h_ref, w_ref, perm_ref, ei, ej, ui, uj, sim, raw, mark, rowmsg, colmsg, losses, tsum, isum_cols, rowacc, factor,
     sa, sb, ra, rb, sa2, sb2, ra2, rb2, inner_out, inner_in,
     gout, g4, hq, gp, gpb, ry, rz, rzb, s_in, s_out, s_back,
 ):
@@ -241,18 +241,16 @@
 
     own_row = y * 4 + x
     own_col = z * 2 + c
-    rowmsg[own_row] = jnp.zeros((16, R), F32)
-
-    def scores(first_slot, last_slot, ky, so_far):
-        y_from = step(y, -ky, 4)
-        rows = pl.ds(pl.multiple_of(y_from * 256, 256), 256)
+
+    def scores(first_slot, last_slot, b, so_far):
+        rows = slice(b * 256, (b + 1) * 256)
         cols = slice(first_slot * R, last_slot * R)
         s = nt(ui[0, rows, :], uj[0, cols, :]) + nt(ui[1, rows, :], uj[1, cols, :])
-        hit = jnp.sum(s * mark[rows, cols], axis=0, keepdims=True)
+        raw[rows, cols] = s
         e = jnp.exp2(EXP2_SCALE * s - EXP2_SCALE)
-        if first_slot == 0 and ky == 0:
+        if first_slot == 0:
             at = lax.broadcasted_iota(jnp.int32, (256, R), 0) - lax.broadcasted_iota(jnp.int32, (256, R), 1)
-            diagonal = at == jnp.where(fetches, xl * R, -ROWS)
+            diagonal = at == jnp.where(fetches, p_me * R - b * 256, -ROWS)
             e = jnp.concatenate([jnp.where(diagonal, 0.0, e[:, 0:R]), e[:, R:]], axis=1)
         sim[rows, cols] = e
         part = e[:, 0:R]
@@ -260,24 +258,17 @@
             part = part + e[:, t * R:(t + 1) * R]
         rowacc[rows, :] = part if first_slot == 0 else rowacc[rows, :] + part
         total = jnp.sum(e, axis=0, keepdims=True)
-        return (total, hit) if so_far is None else (so_far[0] + total, so_far[1] + hit)
+        return total if so_far is None else so_far + total
 
     def hand_in(first_slot, last_slot, so_far):
-        sums, hits = so_far
-        line = hits[:, 0:R]
         for slot in range(first_slot, last_slot):
             t = slot - first_slot
-            colmsg[own_col, pl.ds(step(z, -ORDER[slot], 8), 1), :] = sums[:, t * R:(t + 1) * R]
-            if t:
-                line = line + hits[:, t * R:(t + 1) * R]
-        rowmsg[own_row, 8:9, :] = rowmsg[own_row, 8:9, :] - 0.5 * line
+            colmsg[own_col, pl.ds(step(z, -ORDER[slot], 8), 1), :] = so_far[:, t * R:(t + 1) * R]
 
     @pl.when(jnp.logical_not(fetches))
     def _():
         handed(range(5))
 
-    unit_columns(range(5))
-    so_far = None
     for ky in (0, 1, 3, 2):
         y_from = step(y, -ky, 4)
         if ky == 0:
@@ -288,10 +279,12 @@
             for k in (1, 3, 2):
                 arrived(("xy", k, ky), half_rows(ei, y_from, step(x, -k, 4))[0])
                 arrived(("yx", ky, k), half_rows(ei, y_from, step(x, -k, 4))[1])
-        for half in range(2):
-            rows = pl.ds(pl.multiple_of(y_from * 256 + half * R, R), R)
-            unit(ui, rows, ei[y_from, half], ei[y_from, 2 + half])
-        so_far = scores(0, 5, ky, so_far)
+    for p in range(8):
+        unit(ui, slice(p * R, (p + 1) * R), ei[p // 2, p % 2], ei[p // 2, 2 + p % 2])
+    unit_columns(range(5))
+    so_far = None
+    for b in range(4):
+        so_far = scores(0, 5, b, so_far)
     hand_in(0, 5, so_far)
 
     def hidden_rows(kc, x_):
@@ -324,8 +317,8 @@
 
     unit_columns(range(5, 8))
     so_far = None
-    for ky in (0, 1, 3, 2):
-        so_far = scores(5, 8, ky, so_far)
+    for b in range(4):
+        so_far = scores(5, 8, b, so_far)
     hand_in(5, 8, so_far)
     for p in range(8):
         rowmsg[own_row, p:p + 1, :] = to_rows(rowacc[p * R:(p + 1) * R, :])
@@ -335,6 +328,12 @@
     for ky, kx in PLANE:
         send(("row", ky, kx), rowmsg.at[own_row], rowmsg.at[own_row], dev(dy=ky, dx=kx))
     send_hidden(1)
+    hits = jnp.zeros((1, R), F32)
+    for p in range(8):
+        rows = slice(p * R, (p + 1) * R)
+        hit = jnp.sum(raw[rows, :] * mark[rows, :], axis=0, keepdims=True)
+        for t in range(8):
+            hits = hits - 0.5 * hit[:, t * R:(t + 1) * R]
     for ky, kx in PLANE:
         arrived(("row", ky, kx), rowmsg.at[step(y, -ky, 4) * 4 + step(x, -kx, 4)])
     for kz, kc in COLUMN:
@@ -345,10 +344,8 @@
     for n in range(1, 16):
         all_rows = all_rows + rowmsg[n]
         all_cols = all_cols + colmsg[n]
-    row_total = all_rows[0:8]
-    hit_total = all_rows[8:9]
-    cost = jnp.sum(jnp.log(row_total), axis=0, keepdims=True) - SHARPNESS * (hit_total - 8.0)
-    losses[own_col] = jnp.broadcast_to(cost, (8, R))
+    row_total = all_rows
+    log_sums = jnp.sum(jnp.log(row_total), axis=0, keepdims=True)
 
     inv_rows = 1.0 / row_total
     inv_cols = 1.0 / all_cols
@@ -383,18 +380,18 @@
         for half in range(2):
             v = to_rows(acc[half * R:(half + 1) * R])
             inner_out[y_to, half:half + 1, :] = v
+        inner_out[y_to, 2:3, :] = hits
+        if ky == 0:
+            inner_in[own_row] = inner_out[y]
         for kx in (2, 1, 3, 0):
             if ky or kx:
                 send(
-                    ("in", ky, kx), inner_out.at[y_to], inner_in.at[ky * 4 + kx],
+                    ("in", ky, kx), inner_out.at[y_to], inner_in.at[own_row],
                     dev(dy=ky, dx=kx),
                 )
     for kx in (1, 3, 0):
         for ky in (2, 1, 3):
             send_b(ky, kx)
-    for kz, kc in COLUMN:
-        send(("loss", kz, kc), losses.at[own_col], losses.at[own_col], dev(dz=kz, dc=kc))
-
     flush(0, older)
 
     @pl.when(fetches)
@@ -430,10 +427,11 @@
         send(("rb2", k), sb2.at[k], rb2.at[k], dev(dx=k))
     g_a = total_a(0)
     g_b = total_b(0)
-    inner = inner_out[y]
     for ky, kx in PLANE:
-        arrived(("in", ky, kx), inner_in.at[ky * 4 + kx])
-        inner = inner + inner_in[ky * 4 + kx]
+        arrived(("in", ky, kx), inner_in.at[step(y, -ky, 4) * 4 + step(x, -kx, 4)])
+    inner = inner_in[0]
+    for n in range(1, 16):
+        inner = inner + inner_in[n]
     for k in (2, 1, 3):
         arrived(("ra2", k), ra2.at[k])
         arrived(("rb2", k), rb2.at[k])
@@ -459,6 +457,8 @@
             arrived(("hx", n, kc), hq.at[hidden_rows(kc, 1 - xl), n * 512:(n + 1) * 512])
     near = tn(hq[0:2 * R, :], g4[0:2 * R, :])
     arrived(("g",), g4.at[2 * R:4 * R, :])
+    cost = log_sums - SHARPNESS * (inner[2:3] - 8.0)
+    losses[own_col] = jnp.broadcast_to(cost, (8, R))
     full = near + tn(hq[2 * R:, :], g4[2 * R:, :])
     gp[...] = full
     gpb[...] = full.astype(BF16)
@@ -469,6 +469,8 @@
         for ky in (2, 1, 3):
             send(("gy", ky, kz), gpb.at[piece_at(kz, ky), :], ry.at[ky, kz], dev(dy=ky))
     older = len(sent)
+    for kz, kc in COLUMN:
+        send(("loss", kz, kc), losses.at[own_col], losses.at[own_col], dev(dz=kz, dc=kc))
     for kz in (4, 3, 5, 2, 6, 1, 7, 0):
         piece = gp[piece_at(kz, 0), :]
         for ky in (1, 3, 2):
@@ -477,13 +479,6 @@
         if kz:
             rzb[kz] = piece.astype(BF16)
             send(("gz", kz), rzb.at[kz], rz.at[kz], dev(dz=kz))
-    for kz, kc in COLUMN:
-        arrived(("loss", kz, kc), losses.at[step(z, -kz, 8) * 2 + step(c, kc, 2)])
-    cost = losses[0]
-    for n in range(1, 16):
-        cost = cost + losses[n]
-    loss_ref[...] = jnp.broadcast_to(jnp.sum(cost, axis=1, keepdims=True) * (1.0 / ROWS), (8, R))
-
     flush(0, older)
     for kz in (1, 7, 2, 6, 3, 5, 4):
         arrived(("gz", kz), rz.at[kz])
@@ -532,6 +527,13 @@
         for kz in near_z:
             arrived(("ax", ky, kz), place(1 - xl, c, y_from, step(z, -kz, 8)))
         send(("ac", ky), both(c, y_from), both(c, y_from), dev(dc=1))
+    for kz, kc in COLUMN:
+        arrived(("loss", kz, kc), losses.at[step(z, -kz, 8) * 2 + step(c, kc, 2)])
+    cost = losses[0]
+    for n in range(1, 16):
+        cost = cost + losses[n]
+    loss_ref[...] = jnp.broadcast_to(jnp.sum(cost, axis=1, keepdims=True) * (1.0 / ROWS), (8, R))
+
     for ky in (0, 1, 3, 2):
         there = both(1 - c, step(y, -ky, 4))
         arrived(("ac", ky), there)
@@ -579,7 +581,8 @@
             vmem((2, 1024, 256), BF16),
             vmem((1024, 1024), F32),
             vmem((1024, 1024), F32),
-            vmem((16, 16, R), F32),
+            vmem((1024, 1024), F32),
+            vmem((16, 8, R), F32),
             vmem((16, 8, R), F32),
             vmem((16, 8, R), F32),
             vmem((1, 1024), F32),

time: 72 us -> 71.9 us (level)
  no operation moved by 1% of the time
where the time goes in v7:
time: 71.9 us; the launch traced here: 71.5 us
  Pallas kernels  70.9 us (99%)
    pallas_call x1, Pallas kernels, per_device(): pl.pallas_call(kernel, out_shape=(jax.ShapeDtypeStruct((8, R), F32), jax....  69.4 us
    pallas_call x1, Pallas kernels, per_device(): pl.pallas_call(finish, out_shape=(jax.ShapeDtypeStruct((1, 1), F32), jax....  1.44 us

profile of v7, /device:TPU:1, one launch (start us, length us, event | category | flops | bytes accessed | tf_op | source)
XLA Modules:
  0.0 71.5 jit_solution(12767412427177071170)
XLA Ops:
  0.6 69.4 %shard_map.58 = (f32[8,128]{1,0:T(8,128)S(1)}, f32[128,256]{1,0:T(8,128)S(1)}, bf16[2,4,256,256]{3,2,1,0:T(8,128)(2,1)S(1)}) custom-call(bf16[128,2048]{1,0:T(8,128)(2,1)} %h_hbm.1, bf16[2048,256]{1,0:T(8,128)(2,1)} %w_hbm.1, s32[64,128]{1,0:T(8,128)} %bitcast.4), custom_call_target="tpu_custom_call" | custom-call | tf_op jit(solution)/shard_map/pallas_call | solution.py:565
  70.1 1.4 %shard_map.59 = (f32[1,1]{1,0:T(1,128)}, f32[128,256]{1,0:T(8,128)}, f32[2048,256]{1,0:T(8,128)}) custom-call(f32[8,128]{1,0:T(8,128)S(1)} %get-tuple-element.9.loss_in, f32[128,256]{1,0:T(8,128)S(1)} %get-tuple-element.10.gemb_in, bf16[2048,256]{1,0:T(8,128)(2,1)S(1)} %bitcast.3), custom_call_target="tpu_custom_call" | custom-call | tf_op jit(solution)/shard_map/pallas_call | solution.py:619

commit v8 on v7

--- a/solution.py
+++ b/solution.py
@@ -95,6 +95,11 @@
     def arrived(key, dst):
         copy(key, dst, dst, dev(dc=1)).wait_recv()
 
+    barrier = pltpu.get_barrier_semaphore()
+    peers = [dev(dx=k) for k in (2, 1, 3)] + [dev(dy=k) for k in (2, 1, 3)] + [dev(dz=k) for k in (2, 6, 1, 7)] + [dev(dc=1)]
+    for peer in peers:
+        pl.semaphore_signal(barrier, inc=1, device_id=peer, device_id_type=MESH)
+
     depth = 512
     parts = [slice(k * depth, (k + 1) * depth) for k in range(2048 // depth)]
     loads = []
@@ -104,11 +109,6 @@
     loads.append(pltpu.make_async_copy(perm_hbm, perm_ref, s_in.at[2 * len(parts)]))
     for load in loads:
         load.start()
-
-    barrier = pltpu.get_barrier_semaphore()
-    peers = [dev(dx=k) for k in (2, 1, 3)] + [dev(dy=k) for k in (2, 1, 3)] + [dev(dz=k) for k in (2, 6, 1, 7)] + [dev(dc=1)]
-    for peer in peers:
-        pl.semaphore_signal(barrier, inc=1, device_id=peer, device_id_type=MESH)
 
     total = None
     for n, part in enumerate(parts):

time: 71.9 us -> 71.8 us (level)
  no operation moved by 1% of the time
where the time goes in v8:
time: 71.8 us; the launch traced here: 71.4 us
  Pallas kernels  70.8 us (99%)
    pallas_call x1, Pallas kernels, per_device(): pl.pallas_call(kernel, out_shape=(jax.ShapeDtypeStruct((8, R), F32), jax....  69.3 us
    pallas_call x1, Pallas kernels, per_device(): pl.pallas_call(finish, out_shape=(jax.ShapeDtypeStruct((1, 1), F32), jax....  1.44 us

profile of v8, /device:TPU:1, one launch (start us, length us, event | category | flops | bytes accessed | tf_op | source)
XLA Modules:
  0.0 71.4 jit_solution(9360865573034910461)
XLA Ops:
  0.6 69.3 %shard_map.58 = (f32[8,128]{1,0:T(8,128)S(1)}, f32[128,256]{1,0:T(8,128)S(1)}, bf16[2,4,256,256]{3,2,1,0:T(8,128)(2,1)S(1)}) custom-call(bf16[128,2048]{1,0:T(8,128)(2,1)} %h_hbm.1, bf16[2048,256]{1,0:T(8,128)(2,1)} %w_hbm.1, s32[64,128]{1,0:T(8,128)} %bitcast.4), custom_call_target="tpu_custom_call" | custom-call | tf_op jit(solution)/shard_map/pallas_call | solution.py:565
  70.0 1.4 %shard_map.59 = (f32[1,1]{1,0:T(1,128)}, f32[128,256]{1,0:T(8,128)}, f32[2048,256]{1,0:T(8,128)}) custom-call(f32[8,128]{1,0:T(8,128)S(1)} %get-tuple-element.9.loss_in, f32[128,256]{1,0:T(8,128)S(1)} %get-tuple-element.10.gemb_in, bf16[2048,256]{1,0:T(8,128)(2,1)S(1)} %bitcast.3), custom_call_target="tpu_custom_call" | custom-call | tf_op jit(solution)/shard_map/pallas_call | solution.py:619
